TPU v7x, 128 devices: a whole 4x4x4 slice. The times are simulated.
128 devices in a mesh: rep: 2 (over y_hi), shard: 64 (over z, x, y_lo, core).
Axes of the slice: x: 4, y: 4 (y_hi: 2, y_lo: 2; y = y_hi * 2 + y_lo), z: 4, core: 2. Of those that a mesh axis runs over, the one named last changes fastest.
Arguments:
- hidden_in: bfloat16 [64, 256, 2048], P('shard', 'rep'), may hold values from -6 to 6
- lengths: int32 [64], P('shard'), may hold values from 64 to 256, as said below
- w_query: bfloat16 [2048, 2048], P('shard'), may hold values from -0.1875 to 0.1875
- w_key: bfloat16 [2048, 2048], P('shard'), may hold values from -0.1875 to 0.1875
- w_value: bfloat16 [2048, 2048], P('shard'), may hold values from -0.125 to 0.125
- w_output: bfloat16 [2048, 2048], P('shard'), may hold values from -0.5 to 0.5
- attn_gain: bfloat16 [2048], P('shard'), may hold values from 0.25 to 1.75
- attn_shift: bfloat16 [2048], P('shard'), may hold values from -1.5 to 1.5
- w_up: bfloat16 [2048, 8192], P('shard'), may hold values from -0.125 to 0.125
- w_down: bfloat16 [8192, 2048], P('shard'), may hold values from -0.375 to 0.375
- mlp_gain: bfloat16 [2048], P('shard'), may hold values from 0.25 to 1.75
- mlp_shift: bfloat16 [2048], P('shard'), may hold values from -1.5 to 1.5
- cotangent: bfloat16 [64, 256, 2048], P('shard', 'rep'), may hold values from -6 to 6
Outputs:
- output: bfloat16 [64, 256, 2048], P('shard', 'rep')
- input_grad: float32 [64, 256, 2048], P('shard', 'rep')
- grad_w_query: float32 [2048, 2048], P('shard')
- grad_w_key: float32 [2048, 2048], P('shard')
- grad_w_value: float32 [2048, 2048], P('shard')
- grad_w_output: float32 [2048, 2048], P('shard')
- grad_attn_gain: float32 [2048], P('shard')
- grad_attn_shift: float32 [2048], P('shard')
- grad_w_up: float32 [2048, 8192], P('shard')
- grad_w_down: float32 [8192, 2048], P('shard')
- grad_mlp_gain: float32 [2048], P('shard')
- grad_mlp_shift: float32 [2048], P('shard')
- rms_stats: float32 [3], replicated
Inputs may be any that keep to these rules, and one draw needn't show every extreme that they name: lengths[s] is the number of valid slots of sequence s; slots t with lengths[s] <= t < 256 are padding.
All inputs are finite; a program needn't handle non-finite values.
Results may differ from a plain program's by a relative error of at most 0.019.
Values may be sent and summed in bfloat16 or wider, within the bound.
No kernel may reach another device: no remote copies, remote signals or barrier semaphores. Data moves between devices by JAX's collectives and lax.ppermute only.
A program may use at most 576 MiB of HBM per device.

v0:
```python
import functools
import math

import jax
import jax.numpy as jnp
from jax import lax
from jax.sharding import Mesh
from jax.sharding import PartitionSpec as P

HEAD_DIM = 128
SHARD = ("shard_0", "shard_1", "shard_2", "shard_3")
REP_SHARD = ("rep", "shard_0", "shard_1", "shard_2", "shard_3")


norm_eps = 1e-12
masked_score = -1e30


def sent_together(arrays, axis, dim, along):
    widths = [math.prod(a.shape[along:]) for a in arrays]
    both = jnp.concatenate(
        [a.reshape(*a.shape[:along], w) for a, w in zip(arrays, widths)], axis=along
    )
    out = lax.all_gather(both, axis, axis=dim, tiled=True)
    parts = jnp.split(out, [sum(widths[:k]) for k in range(1, len(widths))], axis=along)
    return tuple((b.reshape(*out.shape[:along], *a.shape[along:]) for a, b in zip(arrays, parts)))


def joined_along(parts, dim):
    shape = list(parts.shape[1:])
    shape[dim] *= parts.shape[0]
    return jnp.moveaxis(parts, 0, dim).reshape(shape)


def copy_for_each(shard, axis):
    length = lax.axis_size(axis)
    return lax.all_to_all(
        jnp.broadcast_to(shard[None], (length, *shard.shape)), axis, 0, 0, tiled=True
    )


def gather_directly(shard, axis, dim):
    return joined_along(copy_for_each(shard, axis), dim)


def in_one_piece(arrays, axis, dim, along):
    both = jnp.concatenate(arrays, axis=along)
    out, at, done = (gather_directly(both, axis, dim), 0, [])
    for a in arrays:
        done.append(lax.slice_in_dim(out, at, at + a.shape[along], axis=along))
        at += a.shape[along]
    return tuple(done)


def by_axis(shard, axes):
    return functools.reduce(lax.psum, axes, shard)


def split_up(shard, dim, length):
    before, after = (shard.shape[:dim], shard.shape[dim + 1 :])
    return jnp.moveaxis(shard.reshape(*before, length, -1, *after), dim, 0)


def summed_on_arrival(shard, axis, dim):
    parts = split_up(shard, dim, lax.axis_size(axis))
    arrived = lax.all_to_all(parts, axis, split_axis=0, concat_axis=0, tiled=True)
    return arrived.astype(jnp.float32).sum(axis=0)


def side_by_side(arrays, axis, dim, along):
    ends, at = ([], 0)
    for a in arrays[:-1]:
        at += a.shape[along]
        ends.append(at)
    both = jnp.concatenate(arrays, axis=along)
    return tuple(jnp.split(summed_on_arrival(both, axis, dim), ends, axis=along))


def in_one_piece_2(arrays, axis, dim, along):
    columns = [a.reshape(*a.shape[:along], -1) for a in arrays]
    both = jnp.concatenate(columns, axis=along)
    out, at, done = (lax.psum_scatter(both, axis, scatter_dimension=dim, tiled=True), 0, [])
    for a, column in zip(arrays, columns):
        share = out[..., at : at + column.shape[along]]
        done.append(share.reshape(*share.shape[:along], *a.shape[along:]))
        at += column.shape[along]
    return tuple(done)


def layer_norm(values, gain_vec, shift_vec):
    center = values - jnp.mean(values, axis=-1, keepdims=True)
    spread = jnp.mean(center * center, axis=-1, keepdims=True)
    return center * lax.rsqrt(spread + norm_eps) * gain_vec + shift_vec


def gelu_tanh(values):
    return jax.nn.gelu(values, approximate=True)


def matmul(left_side, right_side):
    return jnp.dot(left_side, right_side, preferred_element_type=jnp.float32)


def matmul_back(left_side, right_side):
    return lax.dot_general(
        left_side, right_side, (((1,), (1,)), ((), ())), preferred_element_type=jnp.float32
    )


def matmul_over(left_side, right_side):
    return lax.dot_general(
        left_side, right_side, (((0,), (0,)), ((), ())), preferred_element_type=jnp.float32
    )


def owner_order(term, rep_count, shard_count):
    total_rows = term.shape[0]
    blocks = term.reshape(
        (shard_count, rep_count, total_rows // (shard_count * rep_count)) + term.shape[1:]
    )
    return jnp.swapaxes(blocks, 0, 1).reshape(term.shape)


def per_device(
    hidden_in,
    lengths,
    w_query,
    w_key,
    w_value,
    w_output,
    attn_gain,
    attn_shift,
    w_up,
    w_down,
    mlp_gain,
    mlp_shift,
    cotangent,
):
    seq_local, tok_local, width = hidden_in.shape
    rep_count = lax.axis_size("rep")
    shard_count = lax.axis_size(SHARD)
    seq_full = tok_local * rep_count
    head_count = width // HEAD_DIM
    scale = HEAD_DIM ** (-0.5)
    row_count = seq_local * tok_local
    tok_rows = hidden_in.reshape(row_count, width)
    key_pos = jnp.arange(seq_full, dtype=jnp.int32)
    key_open = (key_pos[None, :] < lengths[:, None])[:, None, None, :]
    query_pos = lax.axis_index("rep") * tok_local + jnp.arange(tok_local, dtype=jnp.int32)
    query_valid = (query_pos[None, :] < lengths[:, None]).astype(jnp.float32).reshape(row_count, 1)

    def reorder(term):
        return owner_order(term, rep_count, shard_count)

    attn_full = sent_together(
        (w_query, w_key, w_value, w_output, attn_gain, attn_shift), SHARD, 0, 1
    )
    query_full, key_full, value_full, proj_full, gain_one, shift_one = attn_full
    queries = matmul(tok_rows, query_full).astype(jnp.bfloat16)
    key_local = matmul(tok_rows, key_full).astype(jnp.bfloat16).reshape(seq_local, tok_local, width)
    value_local = (
        matmul(tok_rows, value_full).astype(jnp.bfloat16).reshape(seq_local, tok_local, width)
    )
    key_all, value_all = in_one_piece((key_local, value_local), "rep", 1, 0)
    query_heads = queries.reshape(seq_local, tok_local, head_count, HEAD_DIM)
    key_heads = key_all.reshape(seq_local, seq_full, head_count, HEAD_DIM)
    value_heads = value_all.reshape(seq_local, seq_full, head_count, HEAD_DIM)

    def masked_scores():
        raw_scores = (
            jnp.einsum(
                "sqhd,skhd->shqk", query_heads, key_heads, preferred_element_type=jnp.float32
            )
            * scale
        )
        return jnp.where(key_open, raw_scores, masked_score)

    scores = masked_scores()
    top_score = jnp.max(scores, axis=-1, keepdims=True)
    exponent = jnp.exp(scores - top_score)
    total_exp = jnp.sum(exponent, axis=-1, keepdims=True)
    attn_probs = exponent / total_exp
    log_total = top_score + jnp.log(total_exp)
    probs_low = attn_probs.astype(jnp.bfloat16)
    context = jnp.einsum(
        "shqk,skhd->sqhd", probs_low, value_heads, preferred_element_type=jnp.float32
    )
    context = context.reshape(row_count, width).astype(jnp.bfloat16)
    attn_out = matmul(context, proj_full)
    resid_one = tok_rows.astype(jnp.float32) + attn_out
    normed_one = layer_norm(resid_one, gain_one.astype(jnp.float32), shift_one.astype(jnp.float32))
    hidden_low = normed_one.astype(jnp.bfloat16)
    up_full, down_full, gain_two, shift_two = (
        lax.all_gather(w_up, SHARD, axis=0, tiled=True),
        lax.all_gather(w_down, SHARD, axis=0, tiled=True),
        lax.all_gather(mlp_gain, SHARD, axis=0, tiled=True),
        lax.all_gather(mlp_shift, SHARD, axis=0, tiled=True),
    )
    pre_act = matmul(hidden_low, up_full)
    act_low = gelu_tanh(pre_act).astype(jnp.bfloat16)
    mlp_out = matmul(act_low, down_full)
    resid_two = normed_one + mlp_out
    norm_two_out, norm_two_pull = jax.vjp(
        layer_norm, resid_two, gain_two.astype(jnp.float32), shift_two.astype(jnp.float32)
    )
    output = norm_two_out.astype(jnp.bfloat16).reshape(seq_local, tok_local, width)
    stat_sum = (
        by_axis(jnp.sum(query_valid * resid_one * resid_one), REP_SHARD),
        by_axis(jnp.sum(query_valid * attn_out * attn_out), REP_SHARD),
        by_axis(jnp.sum(query_valid * mlp_out * mlp_out), REP_SHARD),
        by_axis(jnp.sum(query_valid), REP_SHARD),
    )
    rms_stats = jnp.sqrt(jnp.stack([stat_sum[0], stat_sum[1], stat_sum[2]]) / (stat_sum[3] * width))
    grad_out = cotangent.reshape(row_count, width).astype(jnp.float32) * query_valid
    grad_resid_two, grad_gain_two, grad_shift_two = norm_two_pull(grad_out)
    grad_mlp_low = grad_resid_two.astype(jnp.bfloat16)
    grad_down_term = matmul_over(act_low, grad_mlp_low)
    grad_act = matmul_back(grad_mlp_low, down_full)
    gelu_pull = jax.vjp(gelu_tanh, pre_act)[1]
    grad_pre_low = gelu_pull(grad_act)[0].astype(jnp.bfloat16)
    grad_up_term = matmul_over(hidden_low, grad_pre_low)
    grad_normed = grad_resid_two + matmul_back(grad_pre_low, up_full)
    mlp_summed = (
        lax.psum_scatter(reorder(grad_up_term), REP_SHARD, scatter_dimension=0, tiled=True),
        lax.psum_scatter(reorder(grad_down_term), REP_SHARD, scatter_dimension=0, tiled=True),
        lax.psum_scatter(reorder(grad_gain_two), REP_SHARD, scatter_dimension=0, tiled=True),
        lax.psum_scatter(reorder(grad_shift_two), REP_SHARD, scatter_dimension=0, tiled=True),
    )
    query_back, key_back, value_back, proj_back, gain_back, shift_back = attn_full
    norm_one_pull = jax.vjp(
        layer_norm, resid_one, gain_back.astype(jnp.float32), shift_back.astype(jnp.float32)
    )[1]
    grad_resid_one, grad_gain_one, grad_shift_one = norm_one_pull(grad_normed)
    grad_attn_low = grad_resid_one.astype(jnp.bfloat16)
    grad_proj_term = matmul_over(context, grad_attn_low)
    grad_context = (
        matmul_back(grad_attn_low, proj_back)
        .astype(jnp.bfloat16)
        .reshape(seq_local, tok_local, head_count, HEAD_DIM)
    )
    probs_again = jnp.exp(masked_scores() - log_total)
    grad_probs = jnp.einsum(
        "sqhd,skhd->shqk", grad_context, value_heads, preferred_element_type=jnp.float32
    )
    grad_scores = probs_again * (
        grad_probs - jnp.sum(probs_again * grad_probs, axis=-1, keepdims=True)
    )
    scores_low = grad_scores.astype(jnp.bfloat16)
    grad_query_low = (
        (
            jnp.einsum("shqk,skhd->sqhd", scores_low, key_heads, preferred_element_type=jnp.float32)
            * scale
        )
        .astype(jnp.bfloat16)
        .reshape(row_count, width)
    )
    key_part = (
        jnp.einsum("shqk,sqhd->skhd", scores_low, query_heads, preferred_element_type=jnp.float32)
        * scale
    )
    value_part = jnp.einsum(
        "shqk,sqhd->skhd", probs_low, grad_context, preferred_element_type=jnp.float32
    )
    key_sum, value_sum = side_by_side(
        (
            key_part.reshape(seq_local, seq_full, width).astype(jnp.bfloat16),
            value_part.reshape(seq_local, seq_full, width).astype(jnp.bfloat16),
        ),
        "rep",
        1,
        0,
    )
    grad_key_low = key_sum.reshape(row_count, width).astype(jnp.bfloat16)
    grad_value_low = value_sum.reshape(row_count, width).astype(jnp.bfloat16)
    grad_query_term = matmul_over(tok_rows, grad_query_low)
    grad_key_term = matmul_over(tok_rows, grad_key_low)
    grad_value_term = matmul_over(tok_rows, grad_value_low)
    input_grad = (
        grad_resid_one
        + matmul_back(grad_query_low, query_back)
        + matmul_back(grad_key_low, key_back)
        + matmul_back(grad_value_low, value_back)
    )
    attn_summed = in_one_piece_2(
        (
            reorder(grad_query_term),
            reorder(grad_key_term),
            reorder(grad_value_term),
            reorder(grad_proj_term),
            reorder(grad_gain_one),
            reorder(grad_shift_one),
        ),
        REP_SHARD,
        0,
        1,
    )
    final_grads = (
        *tuple(
            (
                part.astype(jnp.float32)
                for part in sent_together(
                    (
                        attn_summed[0].astype(jnp.bfloat16),
                        attn_summed[1].astype(jnp.bfloat16),
                        attn_summed[2].astype(jnp.bfloat16),
                        attn_summed[3].astype(jnp.bfloat16),
                        attn_summed[4].astype(jnp.bfloat16),
                        attn_summed[5].astype(jnp.bfloat16),
                        mlp_summed[0].astype(jnp.bfloat16),
                    ),
                    "rep",
                    0,
                    1,
                )
            )
        ),
        lax.all_gather(mlp_summed[1].astype(jnp.bfloat16), "rep", axis=0, tiled=True).astype(
            jnp.float32
        ),
        lax.all_gather(mlp_summed[2].astype(jnp.bfloat16), "rep", axis=0, tiled=True).astype(
            jnp.float32
        ),
        lax.all_gather(mlp_summed[3].astype(jnp.bfloat16), "rep", axis=0, tiled=True).astype(
            jnp.float32
        ),
    )
    return (
        output,
        input_grad.reshape(seq_local, tok_local, width),
        final_grads[0],
        final_grads[1],
        final_grads[2],
        final_grads[3],
        final_grads[4],
        final_grads[5],
        final_grads[6],
        final_grads[7],
        final_grads[8],
        final_grads[9],
        rms_stats,
    )


def solution(mesh):
    split = Mesh(
        mesh.devices.reshape(mesh.shape["rep"], 4, 4, 2, 2),
        ("rep", "shard_0", "shard_1", "shard_2", "shard_3"),
    )
    return jax.shard_map(
        per_device,
        mesh=split,
        in_specs=(
            P(SHARD, "rep", None),
            P(SHARD),
            P(SHARD, None),
            P(SHARD, None),
            P(SHARD, None),
            P(SHARD, None),
            P(SHARD),
            P(SHARD),
            P(SHARD, None),
            P(SHARD, None),
            P(SHARD),
            P(SHARD),
            P(SHARD, "rep", None),
        ),
        out_specs=(
            P(SHARD, "rep", None),
            P(SHARD, "rep", None),
            P(SHARD, None),
            P(SHARD, None),
            P(SHARD, None),
            P(SHARD, None),
            P(SHARD),
            P(SHARD),
            P(SHARD, None),
            P(SHARD, None),
            P(SHARD),
            P(SHARD),
            P(),
        ),
        check_vma=False,
    )
```

profile of v0, /device:TPU:1, one launch (start us, length us, event | category | flops | bytes accessed | tf_op | source)
XLA Modules:
  0.0 2516.5 jit_solution(8456367566723000488)
XLA Ops:
  16.4 144.4 %all-reduce.13 = (bf16[2048]{0:T(1024)(128)(2,1)S(1)}, bf16[2048]{0:T(1024)(128)(2,1)S(1)}) all-reduce(bf16[2048]{0:T(1024)(128)(2,1)S(1)} %dynamic-update-slice.1, bf16[2048]{0:T(1024)(128)(2,1)S(1)} %dynamic-update-slice), channel_id=1, replica_groups=mesh['rep'=2,'shard_0'=4,'shard_1'=4,'shard_2'=2,'shard_3'=2] {'shard_0'..., use_global_device_ids=true, to_apply=%add.1 | all-reduce | flops 4096 | bytes 16384
  160.8 46.0 %all-gather.5.cloned.1.call-done = bf16[2048,8194]{1,0:T(8,128)(2,1)} async-done(((bf16[32,8194]{1,0:T(8,128)(2,1)}), bf16[2048,8194]{1,0:T(8,128)(2,1)}) %all-gather.5.cloned.1.call-update) | async-done | bytes 33562640 | tf_op jit(solution)/shard_map/all_gather | solution.py:24
  206.8 6.1 fusion.47
  212.9 5.8 fusion.50
  220.9 4.8 all-to-all-start
  228.4 6.0 fusion.41
  234.3 17.7 all-to-all-done
  252.0 2.7 fusion.102
  262.0 5.0 fusion.101
  267.3 150.3 %all-gather.7.cloned.1.call-done = bf16[2048,8192]{1,0:T(8,128)(2,1)} async-done(((bf16[32,8192]{1,0:T(8,128)(2,1)}), bf16[2048,8192]{1,0:T(8,128)(2,1)}) %all-gather.7.cloned.1.call-update) | async-done | bytes 33554448 | tf_op jit(solution)/shard_map/all_gather | solution.py:194
  417.7 17.2 fusion.93
  434.9 176.4 %all-gather.9.cloned.1.call-done = bf16[8192,2048]{1,0:T(8,128)(2,1)} async-done(((bf16[128,2048]{1,0:T(8,128)(2,1)}), bf16[8192,2048]{1,0:T(8,128)(2,1)}) %all-gather.9.cloned.1.call-update) | async-done | bytes 33554448 | tf_op jit(solution)/shard_map/all_gather | solution.py:195
  611.2 18.1 fusion.99
  629.6 3.1 fusion.58
  634.3 18.1 fusion.22
  652.5 23.2 fusion.91
  675.7 44.1 %copy.81 = f32[2,64,16,8192]{3,2,1,0:T(8,128)} copy(f32[2,64,16,8192]{3,2,0,1:T(8,128)} %bitcast.54) | data formatting | bytes 134217728 | tf_op jit(solution)/shard_map/transpose | solution.py:121
  719.8 27.3 %fusion.89 = f32[8192,2048]{1,0:T(8,128)} fusion(f32[128,2048]{1,0:T(8,128)} %get-tuple-element.61, f32[128]{0:T(128)S(1)} %negate_multiply_fusion.1, f32[128,8192]{1,0:T(8,128)} %fusion.93), kind=kOutput, calls=%fused_computation.125 | convolution fusion | flops 4304928768 | bytes 72352256 | tf_op jit(solution)/shard_map/dot_general | solution.py:111
  747.1 44.8 %copy.82 = f32[2,64,64,2048]{3,2,1,0:T(8,128)} copy(f32[2,64,64,2048]{3,2,0,1:T(8,128)} %bitcast.57) | data formatting | bytes 134217728 | tf_op jit(solution)/shard_map/transpose | solution.py:121
  793.9 18.6 multiply_reduce_fusion.1
  815.1 6.5 fusion.44
  827.3 2.3 multiply_reduce_fusion
  831.3 2.8 maximum_bitcast_fusion
  834.1 5.0 all-to-all-start.1
  840.0 9.4 convolution_bitcast_fusion
  849.4 8.1 fusion.77
  857.5 33.5 %all-reduce.12 = (f32[]{:T(128)}, f32[]{:T(128)}, f32[]{:T(128)}, f32[]{:T(128)}) all-reduce(f32[]{:T(128)} %get-tuple-element.25, f32[]{:T(128)} %get-tuple-element.24, f32[]{:T(128)} %get-tuple-element.21, f32[]{:T(128)} %get-tuple-element.56), channel_id=1, replica_groups=mesh['rep'=2,'shard_0'=4,'shard_1'=4,'shard_2'=2,'shard_3'=2] {'rep'}, use_global_device_ids=true, to_apply=%region_34.35 | all-reduce | flops 4 | bytes 32 | tf_op jit(solution)/shard_map/psum | solution.py:56
  891.0 9.3 all-reduce.9
  900.3 10.2 all-reduce.8
  910.5 5.5 all-reduce.11
  916.0 8.0 all-reduce.10
  924.0 12.8 copy.73
  936.8 4.0 copy-done
  940.7 6.1 copy.76
  949.4 2.5 fusion.86
  951.9 7.6 fusion.32
  961.5 2.4 fusion.75
  963.9 6.1 copy.74
  970.0 2.4 fusion.73
  972.4 6.1 copy.75
  978.5 77.8 %concatenate.19 = f32[2048,8194]{1,0:T(8,128)} concatenate(f32[2048,2048]{1,0:T(8,128)} %bitcast.160, f32[2048,2048]{1,0:T(8,128)} %bitcast.162, f32[2048,2048]{1,0:T(8,128)} %bitcast.163, f32[2048,2048]{1,0:T(8,128)} %bitcast.161, f32[2048,1]{1,0:T(8,128)S(1)} %reshape_reshape.8, f32[2048,1]{1,0:T(8,128)S(1)} %reshape_reshape.9), dimensions={1} | concatenate | bytes 134250496 | tf_op jit(solution)/shard_map/concatenate | solution.py:81
  1056.3 806.1 %all-reduce.16 = (bf16[2048,8194]{1,0:T(8,128)(2,1)}, bf16[2048]{0:T(1024)(128)(2,1)S(1)}, bf16[2048]{0:T(1024)(128)(2,1)S(1)}) all-reduce(f32[2048,8194]{1,0:T(8,128)} %concatenate.19, f32[2048]{0:T(1024)S(1)} %reshape.384, ...), channel_id=2, replica_groups=mesh['rep'=2,'shard_0'=4,'shard_1'=4,'shard_2'=2,'shard_3'=2] {'rep','sh..., use_global_device_ids=true, to_apply=%region_14.15.clone | all-reduce | flops 16785408 | bytes 100712448
  1865.5 6.4 fusion.23
  1872.5 6.0 all-reduce.14
  1879.5 7.4 fusion.29
  1886.9 588.7 %reduce-scatter.5.cloned.1.call-done = f32[64,2048]{1,0:T(8,128)} async-done(((f32[8192,2048]{1,0:T(8,128)}), f32[64,2048]{1,0:T(8,128)}) %reduce-scatter.5.cloned.1.call-update) | async-done | bytes 524304 | tf_op jit(solution)/shard_map/reduce_scatter | solution.py:225
  2476.7 7.4 all_gather.33
  2485.2 18.5 all-gather.11.cloned.1.call-done
  (150 shorter events, 50.4 us)
Async XLA Ops:
  7.2 199.6 %all-gather.5.cloned.1.call-start = ((), (), s32[]{:S(2)}) async-start(), calls=%async_computation.4 | async-start | bytes 34611200 | tf_op jit(solution)/shard_map/all_gather | solution.py:24
  10.6 407.1 %all-gather.7.cloned.1.call-start = ((), (), s32[]{:S(2)}) async-start(), calls=%async_computation.5 | async-start | bytes 34078720 | tf_op jit(solution)/shard_map/all_gather | solution.py:194
  11.4 599.9 %all-gather.9.cloned.1.call-start = ((), (), s32[]{:S(2)}) async-start(), calls=%async_computation.6 | async-start | bytes 34078720 | tf_op jit(solution)/shard_map/all_gather | solution.py:195
  160.8 52.1 %copy-start.5 = (bf16[1,128,2048]{2,1,0:T(8,128)(2,1)S(1)}, bf16[1,128,2048]{2,1,0:T(8,128)(2,1)}, u32[]{:S(2)}) copy-start(bf16[1,128,2048]{2,1,0:T(8,128)(2,1)} %param.13) | copy-start | bytes 1572868
  220.9 31.1 %all-to-all-start = ((bf16[2,2,128,2048]{3,2,1,0:T(8,128)(2,1)}), bf16[2,2,128,2048]{3,2,1,0:T(8,128)(2,1)}, u32[]{:S(2)}, u32[]{:S(2)}) async-start(bf16[2,2,128,2048]{3,2,1,0:T(8,128)(2,1)} %broadcast_in_dim.26), calls=%async_computation | async-start | bytes 4194304 | tf_op jit(solution)/shard_map/all_to_all | solution.py:37
  225.7 1637.7 %reduce-scatter.3.cloned.1.call-start = ((), (), s32[]{:S(2)}) async-start(), calls=%async_computation.7 | async-start | bytes 67633152 | tf_op jit(solution)/shard_map/reduce_scatter | solution.py:224
  226.6 406.1 %copy-start.25 = (f32[128]{0:T(128)}, f32[128]{0:T(128)S(1)}, u32[]{:S(2)}) copy-start(f32[128]{0:T(128)S(1)} %get-tuple-element.57) | copy-start | bytes 1540
  234.3 24.5 copy-start.14
  258.8 3.1 copy-start.3
  258.8 1.8 copy-start.9
  259.4 2.5 copy-start.1
  259.4 2.5 copy-start.19
  260.6 1.4 copy-start.23
  262.0 5.0 copy-start.18
  267.3 150.4 %copy-start.27 = (f32[128]{0:T(128)}, f32[128]{0:T(128)S(1)}, u32[]{:S(2)}) copy-start(f32[128]{0:T(128)S(1)} %multiply_reduce_fusion.4) | copy-start | bytes 1540
  434.9 194.7 %copy-start.17 = (bf16[1,128,2048]{2,1,0:T(8,128)(2,1)S(1)}, bf16[1,128,2048]{2,1,0:T(8,128)(2,1)}, u32[]{:S(2)}) copy-start(bf16[1,128,2048]{2,1,0:T(8,128)(2,1)} %param.25) | copy-start | bytes 1572868
  719.8 1755.9 %reduce-scatter.5.cloned.1.call-start = ((), (), s32[]{:S(2)}) async-start(), calls=%async_computation.9 | async-start | bytes 67633152 | tf_op jit(solution)/shard_map/reduce_scatter | solution.py:225
  791.9 0.7 copy-start.29
  791.9 1.9 copy-start.26
  793.9 18.6 copy-start.28
  814.2 1.0 copy-start.10
  815.1 7.7 copy-start.2
  815.1 7.7 copy-start.20
  815.1 7.7 copy-start.24
  822.0 0.8 copy-start.16
  827.3 3.1 copy-start.15
  831.3 8.3 copy-start.4
  834.1 5.9 copy-start.11
  834.1 125.4 %all-to-all-start.1 = ((bf16[2,2,128,2048]{2,3,1,0:T(8,128)(2,1)}), bf16[2,2,128,2048]{2,3,1,0:T(8,128)(2,1)}, u32[]{:S(2)}, u32[]{:S(2)}) async-start(bf16[2,2,128,2048]{2,3,1,0:T(8,128)(2,1)} %maximum_bitcast_fusion), calls=%async_computation.1 | async-start | bytes 4194304 | tf_op jit(solution)/shard_map/all_to_all | solution.py:66
  839.1 1664.6 %all-gather.11.cloned.1.call-start = ((), (), s32[]{:S(2)}) async-start(), calls=%async_computation.8 | async-start | bytes 1585152 | tf_op jit(solution)/shard_map/all_gather | solution.py:24
  840.0 9.4 copy-start.12
  840.0 9.4 copy-start.6
  924.0 16.8 copy-start
  940.7 7.5 copy-start.22
  940.7 7.8 copy-start.21
  940.7 11.2 copy-start.13
  961.5 8.5 copy-start.7
  1056.3 809.2 %copy-start.8 = (bf16[2,128,2048]{1,2,0:T(8,128)(2,1)S(1)}, bf16[2,128,2048]{1,2,0:T(8,128)(2,1)}, u32[]{:S(2)}) copy-start(bf16[2,128,2048]{1,2,0:T(8,128)(2,1)} %copy-done.7) | copy-start | bytes 3145732
  1056.3 809.2 %copy-start.30 = (f32[128,2048]{1,0:T(8,128)S(1)}, f32[128,2048]{1,0:T(8,128)}, u32[]{:S(2)}) copy-start(f32[128,2048]{1,0:T(8,128)} %fusion.32) | copy-start | bytes 3145732
Sparse Core Ops, SparseCore 0:
  10.7 196.0 all-gather.4
  208.5 209.0 all-gather.6
  419.4 191.8 all-gather.8
  719.9 955.2 reduce-scatter.2
  1677.4 798.2 reduce-scatter.4
  2477.2 26.4 all-gather.10
where the time goes:
time: 2530 us; the launch traced here: 2520 us
  blocking collectives  1030 us (41%)
  waiting for transfers between devices  999 us (39%)
  local copies, waits for them, and re-layouts  227 us (9%)
  matrix products  203 us (8%)
  other arithmetic  29.1 us (1%)
    unnamed x3, blocking collectives  957 us
    reduce_scatter x1, waiting for transfers between devices, per_device(): lax.psum_scatter(reorder(grad_down_term), REP_SHARD, scatter_dimension=0,...  589 us
    all_gather x1, waiting for transfers between devices, per_device(): lax.all_gather(w_down, SHARD, axis=0, tiled=True)  176 us
    all_gather x1, waiting for transfers between devices, per_device(): lax.all_gather(w_up, SHARD, axis=0, tiled=True)  150 us
    transpose x10, local copies, waits for them, and re-layouts, owner_order(): return jnp.swapaxes(blocks, 0, 1).reshape(term.shape)  120 us
    concatenate x1, local copies, waits for them, and re-layouts, in_one_piece_2(): both = jnp.concatenate(columns, axis=along)  77.8 us
    dot_general x6, matrix products, matmul_over(): lax.dot_general(left_side, right_side, (((0,), (0,)), ((), ())), preferre...  72.7 us
    psum x5, blocking collectives, by_axis(): return functools.reduce(lax.psum, axes, shard)  66.5 us
  transfers between devices with their start and end apart: 8, of which 6 were waited for; matrix products, arithmetic and copies ran while one was open for 13% of the time, Pallas kernels for 0%

commit v1 on v0

v1 whole, which is shorter than its diff:
```python
import functools

import jax
import jax.numpy as jnp
from jax import lax
from jax.experimental import pallas as pl
from jax.experimental.pallas import tpu as pltpu
from jax.sharding import Mesh
from jax.sharding import PartitionSpec as P

HEAD_DIM = 128
AXES = ("rep", "z", "x", "yl", "c")
SHARD = ("z", "x", "yl", "c")
ZXC = ("z", "x", "c")
Y4 = ("rep", "yl")
Y8 = ("rep", "yl", "c")
norm_eps = 1e-12
masked_score = -1e30
bf16 = jnp.bfloat16
f32 = jnp.float32
i32 = jnp.int32
MIB = 1 << 20
REP, ZZ, XX, YL, CC, LEN = range(6)


def shifted(by, count=4):
    return [(i, (i + by) % count) for i in range(count)]


def xored(by, count):
    return [(i, i ^ by) for i in range(count)]


def from_offset(value, axes, offset):
    return lax.ppermute(value, axes, shifted(-offset))


def to_core(value):
    return lax.ppermute(value, "c", xored(1, 2))


def y_gather(value):
    return [value] + [from_offset(value, Y4, d) for d in (1, 2, 3)]


def x_gather(value):
    return [value] + [from_offset(value, "x", d) for d in (1, 2, 3)]


def sum_parts(parts, axis):
    return [parts[0]] + [lax.ppermute(parts[d], axis, shifted(d)) for d in (1, 2, 3)]


def diagonal(value, to_z, by):
    pairs = []
    for rep in range(2):
        for yl in range(2):
            y = rep * 2 + yl
            at = lambda z: rep * 8 + (z % 4) * 2 + yl
            pairs.append((at(y), at(y + by)) if to_z else (at(y - by), at(y)))
    return lax.ppermute(value, ("rep", "z", "yl"), pairs)


def along_y(value, by):
    pairs = []
    for y in range(4):
        at = lambda v: ((v % 4) // 2) * 8 + y * 2 + v % 2
        pairs.append((at(y), at(y + by)))
    return lax.ppermute(value, ("rep", "z", "yl"), pairs)


def call(kernel, outs, operands, specs, out_specs, grid=(1,), scalars=(), scratch=(), vmem=28):
    return pl.pallas_call(
        kernel,
        grid_spec=pltpu.PrefetchScalarGridSpec(
            num_scalar_prefetch=len(scalars),
            grid=grid,
            in_specs=specs,
            out_specs=out_specs,
            scratch_shapes=scratch,
        ),
        out_shape=outs,
        compiler_params=pltpu.CompilerParams(vmem_limit_bytes=vmem * MIB),
        cost_estimate=pl.CostEstimate(flops=1000, bytes_accessed=1000, transcendentals=0),
    )(*scalars, *operands)


def out(shape, dtype=bf16):
    return jax.ShapeDtypeStruct(shape, dtype)


def whole(shape):
    return pl.BlockSpec(shape, lambda *_: (0,) * len(shape))


def swap_middle(value):
    width = value.shape[1]
    chunk = (lax.broadcasted_iota(i32, value.shape, 1) >> 5) & 3
    ahead = pltpu.roll(value, width - 32, 1)
    behind = pltpu.roll(value, 32, 1)
    return jnp.where(chunk == 1, ahead, jnp.where(chunk == 2, behind, value))


def swap_kernel(tok_ref, out_ref):
    out_ref[...] = swap_middle(tok_ref[...].astype(f32)).astype(bf16)


def prep_kernel(sp, wq_ref, wk_ref, wv_ref, up_ref, g1, s1, g2, s2, keep_ref, send_ref):
    rep, yl = sp[REP], sp[YL]
    s = yl * 2 + sp[CC]
    lane = lax.broadcasted_iota(i32, (1, 128), 1)
    rows = []
    for ref in (g1, s1, g2, s2):
        value = ref[...].astype(f32)
        tiled = jnp.concatenate([value, value, value, value], axis=1)
        rows.append(jnp.where((lane >> 5) == s, tiled, 0.0))
    rows.append(jnp.where(lane == s, sp[LEN].astype(f32), 0.0))
    vec = jnp.concatenate(rows + [jnp.zeros((27, 128), f32)], axis=0).astype(bf16)
    keep_ref[:, 3584:] = vec
    send_ref[:, 3584:] = vec
    for target, dest in ((yl, keep_ref), (1 - yl, send_ref)):
        for i, ref in enumerate((wq_ref, wk_ref, wv_ref)):
            start = pl.multiple_of((rep * 2 + target) * 512, 512)
            block = ref[:, pl.ds(start, 512)]
            for head in range(4):
                dest[:, (head * 3 + i) * 128 : (head * 3 + i + 1) * 128] = block[
                    :, head * 128 : (head + 1) * 128
                ]
        for zx in range(16):
            start = pl.multiple_of(zx * 512 + target * 256, 256)
            block = up_ref[:, pl.ds(start, 256)]
            low = jnp.concatenate([block[:, 0:64], block[:, 128:192]], axis=1)
            high = jnp.concatenate([block[:, 64:128], block[:, 192:256]], axis=1)
            dest[:, 1536 + zx * 128 : 1536 + (zx + 1) * 128] = jnp.where(rep == 0, low, high)


def qkv_piece_kernel(sp, keep_ref, got_ref, out_ref):
    own = pl.ds(pl.multiple_of(sp[YL] * 32, 32), 32)
    other = pl.ds(pl.multiple_of((1 - sp[YL]) * 32, 32), 32)
    out_ref[own, :1536] = keep_ref[:, :1536]
    out_ref[other, :1536] = got_ref[:, :1536]
    vec = (keep_ref[:, 3584:].astype(f32) + got_ref[:, 3584:].astype(f32)).astype(bf16)
    out_ref[0:32, 1536:] = vec
    out_ref[32:64, 1536:] = jnp.zeros_like(vec)


def mlp_piece_kernel(sp, keep_ref, got_ref, down_ref, after1_ref, after2_ref, out_ref):
    own = pl.ds(pl.multiple_of(sp[YL] * 32, 32), 32)
    other = pl.ds(pl.multiple_of((1 - sp[YL]) * 32, 32), 32)
    out_ref[0, own, :] = keep_ref[:, 1536:3584]
    out_ref[0, other, :] = got_ref[:, 1536:3584]
    out_ref[1] = down_ref[pl.ds(pl.multiple_of(sp[REP] * 64, 64), 64), :]


def cat_kernel(t0, t1, t2, t3, after_ref, out_ref):
    for d, ref in enumerate((t0, t1, t2, t3)):
        out_ref[d * 128 : (d + 1) * 128, :] = ref[...]


def out_rows_kernel(sp, own_ref, got_ref, out_ref):
    out_ref[pl.ds(pl.multiple_of(sp[YL] * 32, 32), 32), :] = own_ref[...]
    out_ref[pl.ds(pl.multiple_of((1 - sp[YL]) * 32, 32), 32), :] = got_ref[...]


def proj_kernel(sp, own_ref, other_ref, proj_ref):
    for d in range(4):
        for ref, core in ((own_ref, sp[CC]), (other_ref, 1 - sp[CC])):
            for yl_of in range(2):
                row = pl.multiple_of(((sp[XX] + d) & 3) * 128 + yl_of * 64 + core * 32, 32)
                proj_ref[pl.ds(row, 32), :] = ref[d, yl_of * 32 : (yl_of + 1) * 32, :]


def qkv_kernel(sp, tok_ref, w_ref, vec_in_ref, out_ref, vec_ref, len_ref):
    @pl.when(pl.program_id(0) == 0)
    def _():
        for zx in range(16):
            pair = vec_in_ref[2 * zx].astype(f32) + vec_in_ref[2 * zx + 1].astype(f32)
            vec_ref[:, zx * 128 : (zx + 1) * 128] = pair
        own = (sp[ZZ] * 4 + sp[XX]) * 2
        len_ref[...] = vec_in_ref[own].astype(f32) + vec_in_ref[own + 1].astype(f32)

    weights = w_ref[...].reshape(2048, 256)
    out_ref[...] = jnp.dot(tok_ref[...], weights, preferred_element_type=f32).astype(bf16)


def softmax_of(q, k, open_row):
    raw = lax.dot_general(q, k, (((1,), (1,)), ((), ())), preferred_element_type=f32)
    scores = jnp.where(open_row, raw * (HEAD_DIM**-0.5), masked_score)
    top = jnp.max(scores, axis=-1, keepdims=True)
    exponent = jnp.exp(scores - top)
    return exponent * (1.0 / jnp.sum(exponent, axis=-1, keepdims=True))


def open_keys(sp, lens):
    e, p = pl.program_id(0), pl.program_id(1)
    length = lens[((sp[YL] + p) & 1) * 2 + ((sp[CC] + e) & 1)]
    swap = ((sp[REP] * 2 + sp[YL] + p) & 3) >> 1
    lane = lax.broadcasted_iota(i32, (1, 256), 1)
    position = jnp.where(swap == 1, (lane + 128) & 255, lane)
    return position < length


def head_part(ref, head, i):
    return ref[0, :, 0, :, (head * 3 + i) * 128 : (head * 3 + i + 1) * 128].reshape(256, 128)


def attend_kernel(sp, lens, qkv_ref, ctx_ref):
    open_row = open_keys(sp, lens)
    for head in range(2):
        q, k, v = (head_part(qkv_ref, head, i) for i in range(3))
        probs = softmax_of(q, k, open_row).astype(bf16)
        ctx = jnp.dot(probs, v, preferred_element_type=f32).astype(bf16)
        ctx_ref[0, :, 0, :, head * 128 : (head + 1) * 128] = ctx.reshape(2, 128, 128)


def attend_back_kernel(sp, lens, qkv_ref, own_ref, other_ref, out_ref):
    open_row = open_keys(sp, lens)
    scale = HEAD_DIM**-0.5
    first = pl.program_id(0) == 0
    for head in range(2):
        q, k, v = (head_part(qkv_ref, head, i) for i in range(3))
        cols = slice(head * 128, (head + 1) * 128)
        grad = jnp.where(first, own_ref[:, 0, :, cols], other_ref[:, 0, :, cols]).reshape(256, 128)
        probs = softmax_of(q, k, open_row)
        grad_probs = lax.dot_general(grad, v, (((1,), (1,)), ((), ())), preferred_element_type=f32)
        inner = jnp.sum(probs * grad_probs, axis=-1, keepdims=True)
        grad_scores = (probs * (grad_probs - inner)).astype(bf16)
        grad_q = jnp.dot(grad_scores, k, preferred_element_type=f32) * scale
        over = (((0,), (0,)), ((), ()))
        grad_k = lax.dot_general(grad_scores, q, over, preferred_element_type=f32) * scale
        grad_v = lax.dot_general(probs.astype(bf16), grad, over, preferred_element_type=f32)
        for i, part in enumerate((grad_q, grad_k, grad_v)):
            out_ref[0, :, 0, :, (head * 3 + i) * 128 : (head * 3 + i + 1) * 128] = part.astype(
                bf16
            ).reshape(2, 128, 128)


def group_block(columns):
    return pl.BlockSpec((1, 2, 1, 128, columns), lambda e, p, *_: (e, 0, p, 0, 0))


def to_four(result, refs):
    for d, ref in enumerate(refs):
        ref[...] = result[d * 128 : (d + 1) * 128].astype(bf16)


def out_kernel(sp, own_ref, got_ref, proj_ref, ctx_ref, *refs):
    @pl.when(pl.program_id(0) == 0)
    def _():
        ctx_ref[:, pl.ds(pl.multiple_of(sp[CC] * 256, 256), 256)] = own_ref[0]
        ctx_ref[:, pl.ds(pl.multiple_of((1 - sp[CC]) * 256, 256), 256)] = got_ref[0]

    to_four(jnp.dot(ctx_ref[...], proj_ref[...], preferred_element_type=f32), refs)


def terms_of(refs):
    return sum(r[...].astype(f32) for r in refs[1:]) + refs[0][...].astype(f32)


def valid_rows(sp):
    position = sp[REP] * 128 + lax.broadcasted_iota(i32, (128, 1), 0)
    return (position < sp[LEN]).astype(f32)


def lane_of(values):
    lane = lax.broadcasted_iota(i32, (8, 128), 1)
    total = jnp.zeros((8, 128), f32)
    for i, value in enumerate(values):
        total = jnp.where(lane == i, value, total)
    return total


def normed(values):
    center = values - jnp.mean(values, axis=-1, keepdims=True)
    spread = jnp.mean(center * center, axis=-1, keepdims=True)
    scale = lax.rsqrt(spread + norm_eps)
    return center * scale, scale


def norm_one_kernel(sp, p0, p1, p2, p3, tok_ref, vec_ref, hidden_ref, norm_ref, scale_ref, stat_ref):
    attn = terms_of((p0, p1, p2, p3))
    resid = tok_ref[...].astype(f32) + attn
    norm, scale = normed(resid)
    hidden = norm * vec_ref[0:1, :] + vec_ref[1:2, :]
    hidden_ref[...] = swap_middle(hidden).astype(bf16)
    norm_ref[...] = norm
    scale_ref[...] = jnp.broadcast_to(scale, scale_ref.shape)
    valid = valid_rows(sp)
    stat_ref[...] = lane_of((jnp.sum(valid * (resid * resid)), jnp.sum(valid * (attn * attn))))


def norm_two_kernel(
    sp, p0, p1, p2, p3, norm_ref, vec_ref, cot_ref, stat_ref, out_ref, low_ref, grad_ref, vg_ref, st_ref
):
    mlp = terms_of((p0, p1, p2, p3))
    resid = norm_ref[...] * vec_ref[0:1, :] + vec_ref[1:2, :] + mlp
    norm, scale = normed(resid)
    out_ref[...] = (norm * vec_ref[2:3, :] + vec_ref[3:4, :]).astype(bf16)
    valid = valid_rows(sp)
    grad_out = cot_ref[...].astype(f32) * valid
    vg_ref[0:1, :] = jnp.sum(grad_out * norm, axis=0, keepdims=True)
    vg_ref[1:2, :] = jnp.sum(grad_out, axis=0, keepdims=True)
    e = grad_out * vec_ref[2:3, :]
    mean_e = jnp.mean(e, axis=-1, keepdims=True)
    mean_en = jnp.mean(e * norm, axis=-1, keepdims=True)
    grad = scale * (e - mean_e - norm * mean_en)
    grad_ref[...] = grad
    low_ref[...] = grad.astype(bf16)
    lane = lax.broadcasted_iota(i32, (8, 128), 1)
    more = jnp.where(lane == 2, jnp.sum(valid * (mlp * mlp)), jnp.sum(valid))
    st_ref[...] = jnp.where(lane < 2, stat_ref[...], more)


def norm_one_back_kernel(
    p0, p1, p2, p3, grad2_ref, norm_ref, scale_ref, vec_ref, low_ref, grad_ref, vg_ref
):
    grad = grad2_ref[...] + swap_middle(terms_of((p0, p1, p2, p3)))
    norm = norm_ref[...]
    vg_ref[0:1, :] = jnp.sum(grad * norm, axis=0, keepdims=True)
    vg_ref[1:2, :] = jnp.sum(grad, axis=0, keepdims=True)
    e = grad * vec_ref[0:1, :]
    mean_e = jnp.mean(e, axis=-1, keepdims=True)
    mean_en = jnp.mean(e * norm, axis=-1, keepdims=True)
    back = scale_ref[:, 0:1] * (e - mean_e - norm * mean_en)
    grad_ref[...] = back
    low_ref[...] = back.astype(bf16)


def last_kernel(p0, p1, p2, p3, grad_ref, out_ref):
    out_ref[...] = grad_ref[...] + swap_middle(terms_of((p0, p1, p2, p3)))


def join(refs, all_ref):
    @pl.when(pl.program_id(0) == 0)
    def _():
        for d, ref in enumerate(refs):
            all_ref[d * 128 : (d + 1) * 128, :] = ref[...]


def mlp_kernel(h0, h1, h2, h3, up_ref, down_ref, act_ref, slope_ref, all_ref, *rest):
    refs, total_ref = rest[:4], rest[4]
    join((h0, h1, h2, h3), all_ref)
    v = jnp.dot(all_ref[...], up_ref[...].reshape(2048, 512), preferred_element_type=f32)
    root = 0.7978845608028654
    square = v * v
    t = jnp.tanh(root * v * (1.0 + 0.044715 * square))
    half = 0.5 * (1.0 + t)
    act = (v * half).astype(bf16)
    act_ref[...] = act
    slope = half + 0.5 * v * (1.0 - t * t) * (root * (1.0 + 3 * 0.044715 * square))
    slope_ref[...] = slope.astype(bf16)
    down = down_ref[...].reshape(512, 2048)
    accumulate(jnp.dot(act, down, preferred_element_type=f32), total_ref, refs)


def accumulate(term, total_ref, refs):
    step, last = pl.program_id(0), pl.num_programs(0) - 1

    @pl.when(step == 0)
    def _():
        total_ref[...] = term

    @pl.when((step > 0) & (step < last))
    def _():
        total_ref[...] += term

    @pl.when(step == last)
    def _():
        to_four(total_ref[...] + term, refs)


BACK = (((1,), (1,)), ((), ()))
OVER = (((0,), (0,)), ((), ()))


def mlp_back_kernel(g0, g1, g2, g3, up_ref, down_ref, slope_ref, pre_ref, all_ref, *rest):
    refs, total_ref = rest[:4], rest[4]
    join((g0, g1, g2, g3), all_ref)
    down = down_ref[...].reshape(512, 2048)
    grad = lax.dot_general(all_ref[...], down, BACK, preferred_element_type=f32)
    pre = (grad * slope_ref[...].astype(f32)).astype(bf16)
    pre_ref[...] = pre
    up = up_ref[...].reshape(2048, 512)
    term = lax.dot_general(pre, up, BACK, preferred_element_type=f32)
    accumulate(term, total_ref, refs)


def mlp_terms_kernel(hidden_ref, pre_ref, act_ref, grad_ref, after_ref, out_ref):
    @pl.when(pl.program_id(0) == 0)
    def _():
        r = lax.dot_general(hidden_ref[...], pre_ref[...], OVER, preferred_element_type=f32)
        out_ref[...] = r.astype(bf16).reshape(out_ref.shape)

    @pl.when(pl.program_id(0) == 1)
    def _():
        r = lax.dot_general(act_ref[...], grad_ref[...], OVER, preferred_element_type=f32)
        out_ref[...] = r.astype(bf16).reshape(out_ref.shape)


def ctx_back_kernel(sp, g0, g1, g2, g3, proj_ref, own_ref, other_ref, all_ref):
    for d, ref in enumerate((g0, g1, g2, g3)):
        all_ref[d * 128 : (d + 1) * 128, :] = ref[...]
    for ref, core in ((own_ref, sp[CC]), (other_ref, 1 - sp[CC])):
        weights = proj_ref[pl.ds(pl.multiple_of(core * 256, 256), 256), :]
        ref[...] = lax.dot_general(
            all_ref[...], weights, BACK, preferred_element_type=f32
        ).astype(bf16)


def proj_terms_kernel(sp, ctx_ref, grad_ref, after_ref, mine_ref, send_ref, term_ref):
    term = lax.dot_general(ctx_ref[...], grad_ref[...], OVER, preferred_element_type=f32)
    term_ref[...] = term.astype(bf16)
    for d in range(4):
        for ref, core in ((mine_ref, sp[CC]), (send_ref, 1 - sp[CC])):
            for yl_of in range(2):
                row = pl.multiple_of(((sp[XX] + d) & 3) * 128 + yl_of * 64 + core * 32, 32)
                ref[d, yl_of * 32 : (yl_of + 1) * 32, :] = term_ref[pl.ds(row, 32), :]


def qkv_terms_kernel(sp, tok_ref, grad_ref, vg1_ref, vg2_ref, stat_ref, *rest):
    a_refs, b_refs, term_ref = rest[:4], rest[4:8], rest[8]
    term = lax.dot_general(tok_ref[...], grad_ref[...], OVER, preferred_element_type=f32)
    term_ref[...] = term.astype(bf16)
    dz = (pl.program_id(0) - sp[ZZ]) & 3
    for dx in range(4):
        start = pl.multiple_of(((sp[XX] + dx) & 3) * 128, 128)
        rows = pl.ds(start, 128)
        vec = [vg1_ref[0:2, rows], vg2_ref[0:2, rows], stat_ref[0:4]]
        vec = jnp.concatenate(vec + [jnp.zeros((8, 128), f32)], axis=0).astype(bf16)
        vec = jnp.concatenate([vec, jnp.zeros((16, 256), bf16)], axis=1)
        b_refs[dx][dz] = term_ref[rows, 384:]
        for k in range(4):

            @pl.when(dz == k)
            def _():
                a_refs[k][dx, 0:128, :] = term_ref[rows, :384]
                a_refs[k][dx, 128:144, :] = vec


def proj_add_kernel(mine_ref, got_ref, after_ref, *refs):
    for d, ref in enumerate(refs):
        ref[...] = (mine_ref[d].astype(f32) + got_ref[d].astype(f32)).astype(bf16)


def middle_kernel(*refs):
    a, b, proj = refs[0:4], refs[4:8], refs[8:12]
    outs = refs[13:]
    total = terms_of(a).astype(bf16)
    for d in range(4):
        outs[d][...] = total[d]
    total = terms_of(b).astype(bf16)
    for d in range(4):
        outs[4 + d][...] = total[d]
    outs[8][...] = terms_of(proj).astype(bf16)


def tok_back_kernel(sp, own_ref, got_ref, w_ref, after_ref, *rest):
    refs, cat_ref = rest[:4], rest[4]

    @pl.when(pl.program_id(0) == 0)
    def _():
        cat_ref[:, pl.ds(pl.multiple_of(sp[CC] * 768, 256), 768)] = own_ref[0]
        cat_ref[:, pl.ds(pl.multiple_of((1 - sp[CC]) * 768, 256), 768)] = got_ref[0]

    weights = w_ref[...].reshape(256, 1536)
    to_four(lax.dot_general(cat_ref[...], weights, BACK, preferred_element_type=f32), refs)


def pieces_kernel(sp, *refs):
    a, b, proj = refs[0:4], refs[4:8], refs[8:12]
    outs, near_ref, away_ref, sum_ref, proj_ref = refs[13:21], *refs[21:25]
    sum_ref[:, :384] = terms_of(a).astype(bf16)
    sum_ref[0:128, 384:] = terms_of(b).astype(bf16)
    sum_ref[128:144, 384:] = jnp.zeros((16, 384), bf16)
    for d in range(8):
        yl_of, c_of = sp[YL] ^ ((d >> 1) & 1), sp[CC] ^ (d & 1)
        row = pl.multiple_of(c_of * 64 + yl_of * 32, 32)
        outs[d][0:32, :] = sum_ref[pl.ds(row, 32), :]
        outs[d][32:48, :] = sum_ref[128:144, :]
    proj_ref[...] = terms_of(proj).astype(bf16)
    near_ref[...] = proj_ref[pl.ds(pl.multiple_of(sp[YL] * 32, 32), 32), :]
    away_ref[...] = proj_ref[pl.ds(pl.multiple_of((1 - sp[YL]) * 32, 32), 32), :]


def final_kernel(sp, *refs):
    me = sp[REP] * 4 + sp[YL] * 2 + sp[CC]
    pieces, near, given = refs[:8], refs[8], refs[9:12]
    q_ref, k_ref, v_ref, proj_ref, g1, s1, g2, s2, rms_ref = refs[12:]
    for d in range(8):
        column = pl.multiple_of((me ^ d) * 256, 256)
        for i, ref in enumerate((q_ref, k_ref, v_ref)):
            for head in range(2):
                ref[:, pl.ds(column + head * 128, 128)] = pieces[d][
                    0:32, (head * 3 + i) * 128 : (head * 3 + i + 1) * 128
                ].astype(f32)
    on_diagonal = sp[ZZ] == sp[REP] * 2 + sp[YL]
    proj_ref[...] = jnp.where(on_diagonal, near[...].astype(f32), terms_of(given))
    vec = sum(piece[32:48, :128].astype(f32) for piece in pieces)
    s = sp[YL] * 2 + sp[CC]
    own = jnp.where(s == 0, vec[:, 0:32], vec[:, 32:64])
    own = jnp.where(s == 2, vec[:, 64:96], own)
    own = jnp.where(s == 3, vec[:, 96:128], own)
    for i, ref in enumerate((g1, s1, g2, s2)):
        ref[...] = own[i : i + 1]
    rms_ref[...] = jnp.sqrt(vec[4:5] / (vec[4:5, 3:4] * 2048.0))


def mlp_split_kernel(sp, sum_ref, rep_ref, away_ref):
    rep_ref[0:32, :] = sum_ref[0, pl.ds(pl.multiple_of(sp[YL] * 32, 32), 32), :]
    rep_ref[32:96, :] = sum_ref[1]
    away_ref[...] = sum_ref[0, pl.ds(pl.multiple_of((1 - sp[YL]) * 32, 32), 32), :]


def final_mlp_kernel(sp, own_ref, yl_ref, rep_ref, both_ref, up_ref, down_ref):
    rep, yl = sp[REP], sp[YL]
    mine = own_ref[0, pl.ds(pl.multiple_of(yl * 32, 32), 32), :]
    first_rep, first_yl = rep == 0, yl == 0
    got = {(0, 0): mine, (0, 1): yl_ref[...], (1, 0): rep_ref[0:32], (1, 1): both_ref[...]}
    for yl_of in range(2):
        same = (yl == yl_of)
        near = jnp.where(same, got[0, 0], got[0, 1]).astype(f32)
        far = jnp.where(same, got[1, 0], got[1, 1]).astype(f32)
        low = jnp.where(first_rep, near, far)
        high = jnp.where(first_rep, far, near)
        for zx in range(16):
            for c in range(2):
                src = slice(zx * 128 + c * 64, zx * 128 + c * 64 + 64)
                at = zx * 512 + yl_of * 256 + c * 128
                up_ref[:, at : at + 128] = jnp.concatenate([low[:, src], high[:, src]], axis=1)
    own_rows = pl.ds(pl.multiple_of(rep * 64, 64), 64)
    far_rows = pl.ds(pl.multiple_of((1 - rep) * 64, 64), 64)
    down_ref[own_rows, :] = own_ref[1].astype(f32)
    down_ref[far_rows, :] = rep_ref[32:96].astype(f32)


def per_device(
    hidden_in,
    lengths,
    w_query,
    w_key,
    w_value,
    w_output,
    attn_gain,
    attn_shift,
    w_up,
    w_down,
    mlp_gain,
    mlp_shift,
    cotangent,
):
    rep, z, x, yl, c = (lax.axis_index(a) for a in AXES)
    s, y = yl * 2 + c, rep * 2 + yl
    any_place = pl.BlockSpec(memory_space=pl.ANY)
    tok = hidden_in.reshape(128, 2048)
    cot = cotangent.reshape(128, 2048)
    sp = jnp.stack([rep, z, x, yl, c, lengths[0], lengths[0], lengths[0]]).astype(i32)
    rows = whole((128, 2048))

    keep, send = call(
        prep_kernel,
        [out((32, 3712))] * 2,
        (
            w_query,
            w_key,
            w_value,
            w_up,
            *(v.reshape(1, 32) for v in (attn_gain, attn_shift, mlp_gain, mlp_shift)),
        ),
        [whole((32, 2048))] * 3 + [whole((32, 8192))] + [whole((1, 32))] * 4,
        [whole((32, 3712))] * 2,
        scalars=(sp,),
        vmem=60,
    )
    got = lax.ppermute(send, "yl", xored(1, 2))
    (qkv_piece,) = call(
        qkv_piece_kernel,
        [out((64, 1664))],
        (keep, got),
        [whole((32, 3712))] * 2,
        [whole((64, 1664))],
        scalars=(sp,),
        vmem=16,
    )
    qkv_w = lax.all_gather(qkv_piece, ZXC, axis=0)

    first_yl, on_diagonal = yl == 0, y == z
    out_got = lax.ppermute(w_output, "yl", xored(1, 2))
    (out_piece,) = call(
        out_rows_kernel,
        [out((64, 2048))],
        (w_output, out_got),
        [whole((32, 2048))] * 2,
        [whole((64, 2048))],
        scalars=(sp,),
        vmem=16,
    )
    spread = [diagonal(out_piece, True, by) for by in (1, 2, 3)]
    out_piece = jnp.where(on_diagonal, out_piece, spread[0] + spread[1] + spread[2])
    out_own = jnp.stack(x_gather(out_piece))
    block4 = whole((4, 64, 2048))
    (proj,) = call(
        proj_kernel,
        [out((512, 2048))],
        (out_own, to_core(out_own)),
        [block4, block4],
        [whole((512, 2048))],
        scalars=(sp,),
        vmem=16,
    )

    (tok_swapped,) = call(swap_kernel, [out((128, 2048))], (tok,), [rows], [rows], vmem=16)
    (tok_mine,) = call(
        cat_kernel,
        [out((512, 2048))],
        (*y_gather(tok_swapped), out_own),
        [rows] * 4 + [any_place],
        [whole((512, 2048))],
        vmem=16,
    )
    tok_all = jnp.concatenate([tok_mine, to_core(tok_mine)], axis=0)
    (mlp_piece,) = call(
        mlp_piece_kernel,
        [out((2, 64, 2048))],
        (keep, got, w_down, proj, tok_all),
        [whole((32, 3712))] * 2 + [whole((128, 2048)), any_place, any_place],
        [whole((2, 64, 2048))],
        scalars=(sp,),
        vmem=16,
    )
    mlp_w = lax.all_gather(mlp_piece, ZXC, axis=0)

    qkv_all, vecs, lens = call(
        qkv_kernel,
        [out((1024, 768)), out((16, 2048), f32), out((16, 128), f32)],
        (tok_all, qkv_w, qkv_w),
        [
            whole((1024, 2048)),
            pl.BlockSpec((32, 64, 256), lambda n, sp: (0, 0, sp[CC] * 3 + n)),
            pl.BlockSpec((32, 16, 128), lambda n, sp: (0, 0, 12)),
        ],
        [
            pl.BlockSpec((1024, 256), lambda n, sp: (0, n)),
            whole((16, 2048)),
            whole((16, 128)),
        ],
        grid=(3,),
        scalars=(sp,),
        vmem=60,
    )
    lens = lens[4, :4].astype(i32)
    qkv_all = qkv_all.reshape(2, 2, 2, 128, 768)
    (ctx_all,) = call(
        attend_kernel,
        [out((2, 2, 2, 128, 256))],
        (qkv_all,),
        [group_block(768)],
        [group_block(256)],
        grid=(2, 2),
        scalars=(sp, lens),
        vmem=16,
    )
    ctx_all = ctx_all.reshape(2, 512, 256)
    ctx_got = to_core(ctx_all)
    ctx, *attn_parts = call(
        out_kernel,
        [out((512, 512))] + [out((128, 2048))] * 4,
        (ctx_all, ctx_got, proj),
        [
            pl.BlockSpec((1, 512, 256), lambda n, sp: (0, 0, 0)),
            pl.BlockSpec((1, 512, 256), lambda n, sp: (1, 0, 0)),
            pl.BlockSpec((512, 512), lambda n, sp: (0, n)),
        ],
        [whole((512, 512))] + [pl.BlockSpec((128, 512), lambda n, sp: (0, n))] * 4,
        grid=(4,),
        scalars=(sp,),
    )
    attn_terms = sum_parts(attn_parts, Y4)
    vec_block = whole((16, 2048))
    hidden_low, norm_one, scale_one, stat_one = call(
        norm_one_kernel,
        [out((128, 2048)), out((128, 2048), f32), out((128, 128), f32), out((8, 128), f32)],
        (*attn_terms, tok, vecs),
        [rows] * 5 + [vec_block],
        [rows, rows, whole((128, 128)), whole((8, 128))],
        scalars=(sp,),
        vmem=16,
    )

    four = [rows] * 4
    column = pl.BlockSpec((512, 512), lambda n: (0, n))
    group = whole((512, 2048))
    up_block = pl.BlockSpec((32, 1, 64, 512), lambda n: (0, 0, 0, n))
    down_block = pl.BlockSpec((8, 1, 64, 2048), lambda n: (n, 1, 0, 0))
    total = pltpu.VMEM((512, 2048), f32)
    act, slope, hidden, *mlp_parts = call(
        mlp_kernel,
        [out((512, 2048))] * 3 + [out((128, 2048))] * 4,
        (*y_gather(hidden_low), mlp_w, mlp_w),
        four + [up_block, down_block],
        [column, column, group] + four,
        grid=(4,),
        scratch=[total],
        vmem=60,
    )
    output, grad_low, grad_two, vec_two, stats = call(
        norm_two_kernel,
        [
            out((128, 2048)),
            out((128, 2048)),
            out((128, 2048), f32),
            out((8, 2048), f32),
            out((8, 128), f32),
        ],
        (*sum_parts(mlp_parts, Y4), norm_one, vecs, cot, stat_one),
        four + [rows, vec_block, rows, whole((8, 128))],
        [rows, rows, rows, whole((8, 2048)), whole((8, 128))],
        scalars=(sp,),
        vmem=16,
    )

    pre_grad, grad_mlp, *hidden_parts = call(
        mlp_back_kernel,
        [out((512, 2048))] * 2 + [out((128, 2048))] * 4,
        (*y_gather(grad_low), mlp_w, mlp_w, slope),
        four + [up_block, down_block, column],
        [column, group] + four,
        grid=(4,),
        scratch=[total],
        vmem=60,
    )
    (mlp_terms,) = call(
        mlp_terms_kernel,
        [out((32, 2, 64, 2048))],
        (hidden, pre_grad, act, grad_mlp, hidden_parts[0]),
        [
            pl.BlockSpec((512, 512), lambda w, n: (0, jnp.where(w == 0, n, 3))),
            whole((512, 2048)),
            pl.BlockSpec((512, 512), lambda w, n: (0, jnp.where(w == 1, n, 0))),
            whole((512, 2048)),
            any_place,
        ],
        [pl.BlockSpec((8, 1, 64, 2048), lambda w, n: (n, w, 0, 0))],
        grid=(2, 4),
    )
    mlp_sum = lax.psum_scatter(mlp_terms, ZXC, scatter_dimension=0, tiled=True)
    mlp_sum = mlp_sum.reshape(2, 64, 2048)
    attn_low, grad_one, vec_one = call(
        norm_one_back_kernel,
        [out((128, 2048)), out((128, 2048), f32), out((8, 2048), f32)],
        (*sum_parts(hidden_parts, Y4), grad_two, norm_one, scale_one, vecs),
        four + [rows, rows, whole((128, 128)), vec_block],
        [rows, rows, whole((8, 2048))],
        vmem=16,
    )

    ctx_grad, ctx_grad_send, grad_attn = call(
        ctx_back_kernel,
        [out((512, 256)), out((512, 256)), out((512, 2048))],
        (*y_gather(attn_low), proj),
        four + [whole((512, 2048))],
        [whole((512, 256)), whole((512, 256)), whole((512, 2048))],
        scalars=(sp,),
        vmem=16,
    )
    ctx_grad_got = to_core(ctx_grad_send)
    half_block = pl.BlockSpec((2, 1, 128, 256), lambda e, p, *_: (0, p, 0, 0))
    (qkv_grad,) = call(
        attend_back_kernel,
        [out((2, 2, 2, 128, 768))],
        (qkv_all, ctx_grad.reshape(2, 2, 128, 256), ctx_grad_got.reshape(2, 2, 128, 256)),
        [group_block(768), half_block, half_block],
        [group_block(768)],
        grid=(2, 2),
        scalars=(sp, lens),
        vmem=16,
    )
    qkv_grad = qkv_grad.reshape(2, 512, 768)
    qkv_grad_got = to_core(qkv_grad)

    step_vec = pl.BlockSpec((8, 512), lambda n, sp: (0, n))
    blocks = call(
        qkv_terms_kernel,
        [out((4, 144, 384))] * 4 + [out((4, 128, 384))] * 4,
        (tok_all, qkv_grad.reshape(1024, 768), vec_one, vec_two, stats),
        [
            pl.BlockSpec((1024, 512), lambda n, sp: (0, n)),
            whole((1024, 768)),
            step_vec,
            step_vec,
            whole((8, 128)),
        ],
        [whole((4, 144, 384))] * 4 + [whole((4, 128, 384))] * 4,
        grid=(4,),
        scalars=(sp,),
        scratch=[pltpu.VMEM((512, 768), bf16)],
    )
    proj_block = pl.BlockSpec((4, 64, 512), lambda n, sp: (0, 0, n))
    proj_terms, proj_send = call(
        proj_terms_kernel,
        [out((4, 64, 2048))] * 2,
        (ctx, grad_attn, blocks[0]),
        [whole((512, 512)), pl.BlockSpec((512, 512), lambda n, sp: (0, n)), any_place],
        [proj_block, proj_block],
        grid=(4,),
        scalars=(sp,),
        scratch=[pltpu.VMEM((512, 512), bf16)],
    )
    tok_parts = call(
        tok_back_kernel,
        [out((128, 2048))] * 4,
        (qkv_grad, qkv_grad_got, qkv_w, blocks[0]),
        [
            pl.BlockSpec((1, 512, 768), lambda n, sp: (0, 0, 0)),
            pl.BlockSpec((1, 512, 768), lambda n, sp: (1, 0, 0)),
            pl.BlockSpec((4, 64, 1536), lambda n, sp: (n, 0, 0)),
            any_place,
        ],
        [pl.BlockSpec((128, 256), lambda n, sp: (0, n))] * 4,
        grid=(8,),
        scalars=(sp,),
        scratch=[pltpu.VMEM((512, 1536), bf16)],
    )
    (input_grad,) = call(
        last_kernel,
        [out((128, 2048), f32)],
        (*sum_parts(tok_parts, Y4), grad_one),
        four + [rows],
        [rows],
        vmem=16,
    )

    proj_parts = call(
        proj_add_kernel,
        [out((64, 2048))] * 4,
        (proj_terms, to_core(proj_send), tok_parts[0]),
        [block4, block4, any_place],
        [whole((64, 2048))] * 4,
        vmem=16,
    )
    middle = call(
        middle_kernel,
        [out((144, 384))] * 4 + [out((128, 384))] * 4 + [out((64, 2048))],
        (
            *sum_parts(blocks[:4], "z"),
            *sum_parts(blocks[4:], "x"),
            *sum_parts(proj_parts, "x"),
            input_grad,
        ),
        [whole((4, 144, 384))] * 4
        + [whole((4, 128, 384))] * 4
        + [whole((64, 2048))] * 4
        + [any_place],
        [whole((144, 384))] * 4 + [whole((128, 384))] * 4 + [whole((64, 2048))],
        vmem=16,
    )
    rep_part, up_away = call(
        mlp_split_kernel,
        [out((96, 2048)), out((32, 2048))],
        (mlp_sum,),
        [whole((2, 64, 2048))],
        [whole((96, 2048)), whole((32, 2048))],
        scalars=(sp,),
        vmem=16,
    )
    grad_up, grad_down = call(
        final_mlp_kernel,
        [out((32, 8192), f32), out((128, 2048), f32)],
        (
            mlp_sum,
            lax.ppermute(up_away, Y4, xored(1, 4)),
            lax.ppermute(rep_part, Y4, xored(2, 4)),
            lax.ppermute(up_away, Y4, xored(3, 4)),
        ),
        [whole((2, 64, 2048)), whole((32, 2048)), whole((96, 2048)), whole((32, 2048))],
        [whole((32, 8192)), whole((128, 2048))],
        scalars=(sp,),
        vmem=16,
    )
    *pieces, near, away = call(
        pieces_kernel,
        [out((48, 768))] * 8 + [out((32, 2048))] * 2,
        (
            *sum_parts(middle[:4], "x"),
            *sum_parts(middle[4:8], "z"),
            middle[8],
            *(diagonal(middle[8], False, by) for by in (1, 2, 3)),
            grad_down,
        ),
        [whole((144, 384))] * 4
        + [whole((128, 384))] * 4
        + [whole((64, 2048))] * 4
        + [any_place],
        [whole((48, 768))] * 8 + [whole((32, 2048))] * 2,
        scalars=(sp,),
        scratch=[pltpu.VMEM((144, 768), bf16), pltpu.VMEM((64, 2048), bf16)],
        vmem=16,
    )
    arrived = [pieces[0]] + [lax.ppermute(pieces[d], Y8, xored(d, 8)) for d in range(1, 8)]
    given = [along_y(away, 1), along_y(near, 2), along_y(away, 3)]
    one_row = whole((1, 32))
    grad_q, grad_k, grad_v, grad_proj, g1, s1, g2, s2, rms = call(
        final_kernel,
        [out((32, 2048), f32)] * 4 + [out((1, 32), f32)] * 4 + [out((1, 128), f32)],
        (*arrived, near, *given),
        [whole((48, 768))] * 8 + [whole((32, 2048))] * 4,
        [whole((32, 2048))] * 4 + [one_row] * 4 + [whole((1, 128))],
        scalars=(sp,),
        vmem=16,
    )
    vec_mine = [v.reshape(32) for v in (g1, s1, g2, s2)]
    rms_stats = rms[0, :3]
    return (
        output.reshape(1, 128, 2048),
        input_grad.reshape(1, 128, 2048),
        grad_q,
        grad_k,
        grad_v,
        grad_proj,
        vec_mine[0],
        vec_mine[1],
        grad_up,
        grad_down,
        vec_mine[2],
        vec_mine[3],
        rms_stats,
    )


def solution(mesh):
    split = Mesh(mesh.devices.reshape(2, 4, 4, 2, 2), AXES)
    rows, vec, seq = P(SHARD, None), P(SHARD), P(SHARD, "rep", None)
    return jax.shard_map(
        per_device,
        mesh=split,
        in_specs=(seq, vec, rows, rows, rows, rows, vec, vec, rows, rows, vec, vec, seq),
        out_specs=(seq, seq, rows, rows, rows, rows, vec, vec, rows, rows, vec, vec, P()),
        check_vma=False,
    )
```

time: 2530 us -> 511 us (0.20)
  blocking collectives: 1030 us -> 0 us
  waiting for transfers between devices: 999 us -> 232 us
  matrix products: 203 us -> 0 us
  local copies, waits for them, and re-layouts: 227 us -> 36.2 us
  Pallas kernels: 0 us -> 110 us
  starting transfers between devices: 10.6 us -> 107 us
  other arithmetic: 29.1 us -> 1.41 us
    unnamed x3 -> x0, blocking collectives: 957 us -> none
    reduce_scatter x2 -> x1, waiting for transfers between devices: 589 us -> 11.3 us  [per_device(): mlp_sum = lax.psum_scatter(mlp_terms, ZXC, scatter_dimension=0, tiled=True)]
    all_gather x4 -> x2, waiting for transfers between devices: 391 us -> 0.02 us  [the longest x1 0.02 us: per_device(): qkv_w = lax.all_gather(qkv_piece, ZXC, axis=0)]
    ppermute x0 -> x69, waiting for transfers between devices: none -> 221 us  [the longest x27 97.5 us: sum_parts(): lax.ppermute(parts[d], axis, shifted(d))]
    dot_general x24 -> x0, matrix products: 203 us -> none  [the longest x6 72.7 us: matmul_over(): lax.dot_general(left_side, right_side, (((0,), (0,)), ((), ())), preferre...]
    transpose x10 -> x0, local copies, waits for them, and re-layouts: 120 us -> none  [owner_order(): return jnp.swapaxes(blocks, 0, 1).reshape(term.shape)]
    pallas_call x0 -> x28, Pallas kernels: none -> 110 us  [call(): pl.pallas_call(kernel, grid_spec=pltpu.PrefetchScalarGridSpec(num_scalar_...]
    ppermute x0 -> x69, starting transfers between devices: none -> 107 us  [the longest x27 40.1 us: sum_parts(): lax.ppermute(parts[d], axis, shifted(d))]
  transfers between devices with their start and end apart: 8 -> 72, of which waited for: 6 -> 37; matrix products, arithmetic and copies ran while one was open for 13% -> 0% of each run, Pallas kernels for 0% -> 11%
where the time goes in v1:
time: 511 us; the launch traced here: 502 us
  waiting for transfers between devices  232 us (45%)
  Pallas kernels  110 us (22%)
  starting transfers between devices  107 us (21%)
  local copies, waits for them, and re-layouts  36.2 us (7%)
  between operations  15.4 us (3%)
    pallas_call x28, Pallas kernels, call(): pl.pallas_call(kernel, grid_spec=pltpu.PrefetchScalarGridSpec(num_scalar_...  110 us
    ppermute x27, waiting for transfers between devices, sum_parts(): lax.ppermute(parts[d], axis, shifted(d))  97.5 us
    ppermute x15, waiting for transfers between devices, from_offset(): return lax.ppermute(value, axes, shifted(-offset))  86.5 us
    ppermute x27, starting transfers between devices, sum_parts(): lax.ppermute(parts[d], axis, shifted(d))  40.1 us
    unnamed x110, local copies, waits for them, and re-layouts  35.1 us
    ppermute x15, starting transfers between devices, from_offset(): return lax.ppermute(value, axes, shifted(-offset))  21.9 us
    ppermute x6, waiting for transfers between devices, diagonal(): return lax.ppermute(value, ('rep', 'z', 'yl'), pairs)  12.4 us
    ppermute x6, starting transfers between devices, diagonal(): return lax.ppermute(value, ('rep', 'z', 'yl'), pairs)  12.3 us
  transfers between devices with their start and end apart: 72, of which 37 were waited for; matrix products, arithmetic and copies ran while one was open for 0% of the time, Pallas kernels for 11%

profile of v1, /device:TPU:1, one launch (start us, length us, event | category | flops | bytes accessed | tf_op | source)
XLA Modules:
  0.0 501.5 jit_solution(3786191516264389855)
XLA Ops:
  8.5 2.8 shard_map.231
  13.4 5.3 %collective-permute-done.11.got_ref = bf16[32,3712]{1,0:T(8,128)(2,1)S(1)} collective-permute-done((bf16[32,3712]{1,0:T(8,128)(2,1)}, bf16[32,3712]{1,0:T(8,128)(2,1)S(1)}, u32[]{:S(2)}, u32[]{:S(2)}) %collective-permute-start.11) | collective-permute-done | bytes 237600 | tf_op jit(solution)/shard_map/ppermute | solution.py:574
  28.0 5.8 %collective-permute-start.6 = (bf16[64,2048]{1,0:T(8,128)(2,1)S(1)}, bf16[64,2048]{1,0:T(8,128)(2,1)S(1)}, u32[]{:S(2)}, u32[]{:S(2)}) collective-permute-start(bf16[64,2048]{1,0:T(8,128)(2,1)S(1)} %shard_map.229), channel_id=1, source_target_pairs={{0,48},{18,2},{96,80},{114,98},{1,49},{19,3},{97,81},{115,99},{4,5... | collective-permute-start | bytes 786440 | tf_op jit(solution)/shard_map/ppermute | solution.py:61
  40.4 7.9 %collective-permute-done.4 = bf16[64,2048]{1,0:T(8,128)(2,1)S(1)} collective-permute-done((bf16[64,2048]{1,0:T(8,128)(2,1)S(1)}, bf16[64,2048]{1,0:T(8,128)(2,1)S(1)}, u32[]{:S(2)}, u32[]{:S(2)}) %collective-permute-start.4) | collective-permute-done | bytes 262176 | tf_op jit(solution)/shard_map/ppermute | solution.py:61
  56.4 8.4 %collective-permute-done.8 = bf16[64,2048]{1,0:T(8,128)(2,1)S(1)} collective-permute-done((bf16[64,2048]{1,0:T(8,128)(2,1)S(1)}, bf16[64,2048]{1,0:T(8,128)(2,1)S(1)}, u32[]{:S(2)}, u32[]{:S(2)}) %collective-permute-start.8) | collective-permute-done | bytes 262176 | tf_op jit(solution)/shard_map/ppermute | solution.py:35
  64.8 5.5 %collective-permute-done.7 = bf16[64,2048]{1,0:T(8,128)(2,1)S(1)} collective-permute-done((bf16[64,2048]{1,0:T(8,128)(2,1)S(1)}, bf16[64,2048]{1,0:T(8,128)(2,1)S(1)}, u32[]{:S(2)}, u32[]{:S(2)}) %collective-permute-start.7) | collective-permute-done | bytes 262176 | tf_op jit(solution)/shard_map/ppermute | solution.py:35
  70.4 3.5 collective-permute-done.2.t3
  75.4 3.0 collective-permute-start.10
  78.5 6.1 %collective-permute-done.13.other_ref = bf16[4,64,2048]{2,1,0:T(8,128)(2,1)S(1)} collective-permute-done((bf16[4,64,2048]{2,1,0:T(8,128)(2,1)S(1)}, bf16[4,64,2048]{2,1,0:T(8,128)(2,1)S(1)}, u32[]{:S(2)}, u32[]{:S(2)}) %collective-permute-start.13) | collective-permute-done | bytes 1048608 | tf_op jit(solution)/shard_map/ppermute | solution.py:39
  90.0 8.1 %shard_map.233 = (bf16[1024,768]{1,0:T(8,128)(2,1)}, f32[16,2048]{1,0:T(8,128)}, f32[16,128]{1,0:T(8,128)}) custom-call(s32[8]{0:T(128)} %stack.38.sp, bf16[1024,2048]{1,0:T(8,128)(2,1)} %copy-done, bf16[32,64,1664]{2,1,0:T(8,128)(2,1)} %bitcast.34, bf16[32,64,1664]{2,1,0:T(8,128)(2,1)} %bitcast.35), custom_call_target="tpu_custom_call" | custom-call | flops 1000 | bytes 1000 | tf_op jit(solution)/shard_map/pallas_call | solution.py:73
  100.2 4.4 shard_map.234
  106.7 2.7 shard_map.236
  113.5 11.1 %collective-permute-done.14.p1 = bf16[128,2048]{1,0:T(8,128)(2,1)S(1)} collective-permute-done((bf16[128,2048]{1,0:T(8,128)(2,1)S(1)}, bf16[128,2048]{1,0:T(8,128)(2,1)S(1)}, u32[]{:S(2)}, u32[]{:S(2)}) %collective-permute-start.14) | collective-permute-done | bytes 524320 | tf_op jit(solution)/shard_map/ppermute | solution.py:51
  124.5 10.2 %collective-permute-done.15.p2 = bf16[128,2048]{1,0:T(8,128)(2,1)S(1)} collective-permute-done((bf16[128,2048]{1,0:T(8,128)(2,1)S(1)}, bf16[128,2048]{1,0:T(8,128)(2,1)S(1)}, u32[]{:S(2)}, u32[]{:S(2)}) %collective-permute-start.15) | collective-permute-done | bytes 524320 | tf_op jit(solution)/shard_map/ppermute | solution.py:51
  142.3 9.8 %collective-permute-done.19.h3 = bf16[128,2048]{1,0:T(8,128)(2,1)S(1)} collective-permute-done((bf16[128,2048]{1,0:T(8,128)(2,1)S(1)}, bf16[128,2048]{1,0:T(8,128)(2,1)S(1)}, u32[]{:S(2)}, u32[]{:S(2)}) %collective-permute-start.19) | collective-permute-done | bytes 524320 | tf_op jit(solution)/shard_map/ppermute | solution.py:35
  152.1 12.7 %collective-permute-done.18.h2 = bf16[128,2048]{1,0:T(8,128)(2,1)S(1)} collective-permute-done((bf16[128,2048]{1,0:T(8,128)(2,1)S(1)}, bf16[128,2048]{1,0:T(8,128)(2,1)S(1)}, u32[]{:S(2)}, u32[]{:S(2)}) %collective-permute-start.18) | collective-permute-done | bytes 524320 | tf_op jit(solution)/shard_map/ppermute | solution.py:35
  165.5 18.5 %shard_map.239 = (bf16[512,2048]{1,0:T(8,128)(2,1)}, bf16[512,2048]{1,0:T(8,128)(2,1)}, bf16[512,2048]{1,0:T(8,128)(2,1)}, bf16[128,2048]{1,0:T(8,128)(2,1)}, bf...) custom-call(bf16[128,2048]{1,0:T(8,128)(2,1)} %copy-done.24, ...), custom_call_target="tpu_custom_call" | custom-call | flops 1000 | bytes 1000 | tf_op jit(solution)/shard_map/pallas_call | solution.py:73
  187.9 9.8 %collective-permute-done.20.p1 = bf16[128,2048]{1,0:T(8,128)(2,1)S(1)} collective-permute-done((bf16[128,2048]{1,0:T(8,128)(2,1)}, bf16[128,2048]{1,0:T(8,128)(2,1)S(1)}, u32[]{:S(2)}, u32[]{:S(2)}) %collective-permute-start.20) | collective-permute-done | bytes 524320 | tf_op jit(solution)/shard_map/ppermute | solution.py:51
  197.7 12.5 %collective-permute-done.21.p2 = bf16[128,2048]{1,0:T(8,128)(2,1)S(1)} collective-permute-done((bf16[128,2048]{1,0:T(8,128)(2,1)}, bf16[128,2048]{1,0:T(8,128)(2,1)S(1)}, u32[]{:S(2)}, u32[]{:S(2)}) %collective-permute-start.21) | collective-permute-done | bytes 524320 | tf_op jit(solution)/shard_map/ppermute | solution.py:51
  220.7 9.6 %collective-permute-done.25.g3 = bf16[128,2048]{1,0:T(8,128)(2,1)S(1)} collective-permute-done((bf16[128,2048]{1,0:T(8,128)(2,1)S(1)}, bf16[128,2048]{1,0:T(8,128)(2,1)S(1)}, u32[]{:S(2)}, u32[]{:S(2)}) %collective-permute-start.25) | collective-permute-done | bytes 524320 | tf_op jit(solution)/shard_map/ppermute | solution.py:35
  230.3 12.8 %collective-permute-done.24.g2 = bf16[128,2048]{1,0:T(8,128)(2,1)S(1)} collective-permute-done((bf16[128,2048]{1,0:T(8,128)(2,1)S(1)}, bf16[128,2048]{1,0:T(8,128)(2,1)S(1)}, u32[]{:S(2)}, u32[]{:S(2)}) %collective-permute-start.24) | collective-permute-done | bytes 524320 | tf_op jit(solution)/shard_map/ppermute | solution.py:35
  244.7 16.3 %shard_map.241 = (bf16[512,2048]{1,0:T(8,128)(2,1)}, bf16[512,2048]{1,0:T(8,128)(2,1)}, bf16[128,2048]{1,0:T(8,128)(2,1)}, bf16[128,2048]{1,0:T(8,128)(2,1)}, bf...) custom-call(bf16[128,2048]{1,0:T(8,128)(2,1)} %copy-done.25, bf16[128,2048]{1,0:T(8,128)(2,1)} %copy-done.52, ...), custom_call_target="tpu_custom_call" | custom-call | flops 1000 | bytes 1000 | tf_op jit(solution)/shard_map/pallas_call | solution.py:73
  268.4 12.0 %shard_map.251 = bf16[32,2,64,2048]{3,2,1,0:T(8,128)(2,1)S(1)} custom-call(bf16[512,2048]{1,0:T(8,128)(2,1)S(1)} %copy-done.7, bf16[512,2048]{1,0:T(8,128)(2,1)S(1)} %copy-done.8, bf16[512,2048]{1,0:T(8,128)(2,1)S(1)} %copy-done.6, bf16[512,2048]{1,0:T(8,128)(2,1)S(1)} %copy-done.9, bf16[128,2048]{1,0:T(8,128)(2,1)S(1)} %copy-done.10), custom_call_target="tpu_custom_call" | custom-call | flops 1000 | bytes 1000 | tf_op jit(solution)/shard_map/pallas_call | solution.py:73
  280.4 5.8 %copy-done.2 = bf16[32,2,64,2048]{3,2,1,0:T(8,128)(2,1)} copy-done((bf16[32,2,64,2048]{3,2,1,0:T(8,128)(2,1)}, bf16[32,2,64,2048]{3,2,1,0:T(8,128)(2,1)S(1)}, u32[]{:S(2)}) %copy-start.2) | copy-done | bytes 16777240
  289.4 10.4 %collective-permute-done.26.p1 = bf16[128,2048]{1,0:T(8,128)(2,1)S(1)} collective-permute-done((bf16[128,2048]{1,0:T(8,128)(2,1)}, bf16[128,2048]{1,0:T(8,128)(2,1)S(1)}, u32[]{:S(2)}, u32[]{:S(2)}) %collective-permute-start.26) | collective-permute-done | bytes 524320 | tf_op jit(solution)/shard_map/ppermute | solution.py:51
  299.8 12.5 %collective-permute-done.27.p2 = bf16[128,2048]{1,0:T(8,128)(2,1)S(1)} collective-permute-done((bf16[128,2048]{1,0:T(8,128)(2,1)}, bf16[128,2048]{1,0:T(8,128)(2,1)S(1)}, u32[]{:S(2)}, u32[]{:S(2)}) %collective-permute-start.27) | collective-permute-done | bytes 524320 | tf_op jit(solution)/shard_map/ppermute | solution.py:51
  318.4 3.3 collective-permute-start.30
  321.7 10.0 %collective-permute-done.31.g3 = bf16[128,2048]{1,0:T(8,128)(2,1)S(1)} collective-permute-done((bf16[128,2048]{1,0:T(8,128)(2,1)S(1)}, bf16[128,2048]{1,0:T(8,128)(2,1)S(1)}, u32[]{:S(2)}, u32[]{:S(2)}) %collective-permute-start.31) | collective-permute-done | bytes 524320 | tf_op jit(solution)/shard_map/ppermute | solution.py:35
  331.7 12.8 %collective-permute-done.30.g2 = bf16[128,2048]{1,0:T(8,128)(2,1)S(1)} collective-permute-done((bf16[128,2048]{1,0:T(8,128)(2,1)S(1)}, bf16[128,2048]{1,0:T(8,128)(2,1)S(1)}, u32[]{:S(2)}, u32[]{:S(2)}) %collective-permute-start.30) | collective-permute-done | bytes 524320 | tf_op jit(solution)/shard_map/ppermute | solution.py:35
  348.9 6.0 %shard_map.244 = bf16[2,2,2,128,768]{4,3,2,1,0:T(8,128)(2,1)S(1)} custom-call(s32[8]{0:T(128)S(1)} %copy-done.46, s32[4]{0:T(128)S(1)} %convert_bitcast_fusion.lens, bf16[2,2,2,128,768]{4,3,2,1,0:T(8,128)(2,1)S(1)} %bitcast.43, bf16[2,2,128,256]{3,2,1,0:T(8,128)(2,1)S(1)} %bitcast.52, bf16[2,2,128,256]{3,2,1,0:T(8,128)(2,1)S(1)} %bitcast.53), custom_call_target="tpu_custom_call" | custom-call | flops 1000 | bytes 1000 | tf_op jit(solution)/shard_map/pallas_call | solution.py:73
  355.5 6.4 %shard_map.245 = (bf16[4,144,384]{2,1,0:T(8,128)(2,1)S(1)}, bf16[4,144,384]{2,1,0:T(8,128)(2,1)S(1)}, bf16[4,144,384]{2,1,0:T(8,128)(2,1)S(1)}, bf16[4,144,384]{...) custom-call(s32[8]{0:T(128)S(1)} %copy-done.46, ...), custom_call_target="tpu_custom_call" | custom-call | flops 1000 | bytes 1000 | tf_op jit(solution)/shard_map/pallas_call | solution.py:73
  361.9 2.9 shard_map.248
  365.7 3.6 collective-permute-start.41
  373.7 6.9 %shard_map.246 = (bf16[128,2048]{1,0:T(8,128)(2,1)S(1)}, bf16[128,2048]{1,0:T(8,128)(2,1)S(1)}, bf16[128,2048]{1,0:T(8,128)(2,1)S(1)}, bf16[128,2048]{1,0:T(8,128)(2,1)}) custom-call(s32[8]{0:T(128)S(1)} %copy-done.46, bf16[2,512,768]{2,1,0:T(8,128)(2,1)S(1)} %bitcast.41, bf16[2,512,768]{2,1,0:T(8,128)(2,1)S(1)} %collective-permute-done.33.got_ref, ...), custom_call_target="tpu_custom_call" | custom-call | flops 1000 | bytes 1000 | tf_op jit(solution)/shard_map/pallas_call | solution.py:73
  380.6 4.9 collective-permute-done.40.refs_5_
  385.5 10.3 %collective-permute-done.41.refs_6_ = bf16[4,128,384]{2,1,0:T(8,128)(2,1)S(1)} collective-permute-done((bf16[4,128,384]{2,1,0:T(8,128)(2,1)S(1)}, bf16[4,128,384]{2,1,0:T(8,128)(2,1)S(1)}, u32[]{:S(2)}, u32[]{:S(2)}) %collective-permute-start.41) | collective-permute-done | bytes 393248 | tf_op jit(solution)/shard_map/ppermute | solution.py:51
  396.5 2.8 collective-permute-start.35
  405.0 10.9 %collective-permute-done.38.refs_2_ = bf16[4,144,384]{2,1,0:T(8,128)(2,1)S(1)} collective-permute-done((bf16[4,144,384]{2,1,0:T(8,128)(2,1)S(1)}, bf16[4,144,384]{2,1,0:T(8,128)(2,1)S(1)}, u32[]{:S(2)}, u32[]{:S(2)}) %collective-permute-start.38) | collective-permute-done | bytes 442400 | tf_op jit(solution)/shard_map/ppermute | solution.py:51
  416.7 2.7 collective-permute-start.46
  419.4 11.3 %reduce-scatter.2.cloned.1.call-done = bf16[1,2,64,2048]{3,2,1,0:T(8,128)(2,1)} async-done(((bf16[32,2,64,2048]{3,2,1,0:T(8,128)(2,1)}), bf16[1,2,64,2048]{3,2,1,0:T(8,128)(2,1)}) %reduce-scatter.2.cloned.1.call-update) | async-done | bytes 524304 | tf_op jit(solution)/shard_map/reduce_scatter | solution.py:745
  432.5 2.8 shard_map.247.refs_12_
  440.6 2.8 collective-permute-start.58
  453.8 3.8 collective-permute-done.56.yl_ref
  457.5 4.8 collective-permute-start.48
  469.2 3.6 collective-permute-start.59
  474.5 3.2 collective-permute-start.62
  477.8 5.1 %collective-permute-start.67 = (bf16[32,2048]{1,0:T(8,128)(2,1)S(1)}, bf16[32,2048]{1,0:T(8,128)(2,1)S(1)}, u32[]{:S(2)}, u32[]{:S(2)}) collective-permute-start(bf16[32,2048]{1,0:T(8,128)(2,1)S(1)} %get-tuple-element.177.refs_8_), channel_id=1, source_target_pairs={{0,64},{18,82},{96,32},{114,50},{1,65},{19,83},{97,33},{115,51},{4... | collective-permute-start | bytes 393224 | tf_op jit(solution)/shard_map/ppermute | solution.py:69
  485.7 3.2 collective-permute-start.65
  (244 shorter events, 134.5 us)
Async XLA Ops:
  7.2 82.8 %all-gather.5.cloned.1.call-start = ((), (), s32[]{:S(2)}) async-start(), calls=%async_computation.2 | async-start | bytes 7028736 | tf_op jit(solution)/shard_map/all_gather | solution.py:584
  21.6 143.9 %all-gather.7.cloned.1.call-start = ((), (), s32[]{:S(2)}) async-start(), calls=%async_computation.3 | async-start | bytes 17301504 | tf_op jit(solution)/shard_map/all_gather | solution.py:630
  35.2 13.1 %collective-permute-start.4 = (bf16[64,2048]{1,0:T(8,128)(2,1)S(1)}, bf16[64,2048]{1,0:T(8,128)(2,1)S(1)}, u32[]{:S(2)}, u32[]{:S(2)}) collective-permute-start(bf16[64,2048]{1,0:T(8,128)(2,1)S(1)} %shard_map.229), channel_id=1, source_target_pairs={{0,16},{18,34},{96,112},{114,66},{1,17},{19,35},{97,113},{115,67},... | collective-permute-start | bytes 786440 | tf_op jit(solution)/shard_map/ppermute | solution.py:61
  50.0 23.9 %collective-permute-start.2 = (bf16[128,2048]{1,0:T(8,128)(2,1)S(1)}, bf16[128,2048]{1,0:T(8,128)(2,1)S(1)}, u32[]{:S(2)}, u32[]{:S(2)}) collective-permute-start(bf16[128,2048]{1,0:T(8,128)(2,1)S(1)} %shard_map.228.t0), channel_id=1, source_target_pairs={{0,2},{2,64},{64,66},{66,0},{1,3},{3,65},{65,67},{67,1},{4,6},{6,6... | collective-permute-start | bytes 1572872 | tf_op jit(solution)/shard_map/ppermute | solution.py:35
  50.1 23.9 %collective-permute-start.1 = (bf16[128,2048]{1,0:T(8,128)(2,1)S(1)}, bf16[128,2048]{1,0:T(8,128)(2,1)S(1)}, u32[]{:S(2)}, u32[]{:S(2)}) collective-permute-start(bf16[128,2048]{1,0:T(8,128)(2,1)S(1)} %shard_map.228.t0), channel_id=1, source_target_pairs={{0,64},{2,66},{64,0},{66,2},{1,65},{3,67},{65,1},{67,3},{4,68},{6,... | collective-permute-start | bytes 1572872 | tf_op jit(solution)/shard_map/ppermute | solution.py:35
  50.2 25.1 %collective-permute-start = (bf16[128,2048]{1,0:T(8,128)(2,1)S(1)}, bf16[128,2048]{1,0:T(8,128)(2,1)S(1)}, u32[]{:S(2)}, u32[]{:S(2)}) collective-permute-start(bf16[128,2048]{1,0:T(8,128)(2,1)S(1)} %shard_map.228.t0), channel_id=1, source_target_pairs={{0,66},{2,0},{64,2},{66,64},{1,67},{3,1},{65,3},{67,65},{4,70},{6,... | collective-permute-start | bytes 1572872 | tf_op jit(solution)/shard_map/ppermute | solution.py:35
  52.8 12.0 %collective-permute-start.8 = (bf16[64,2048]{1,0:T(8,128)(2,1)S(1)}, bf16[64,2048]{1,0:T(8,128)(2,1)S(1)}, u32[]{:S(2)}, u32[]{:S(2)}) collective-permute-start(bf16[64,2048]{1,0:T(8,128)(2,1)S(1)} %add_select_fusion), channel_id=1, source_target_pairs={{0,8},{4,12},{8,0},{12,4},{1,9},{5,13},{9,1},{13,5},{2,10},{6,14},... | collective-permute-start | bytes 786440 | tf_op jit(solution)/shard_map/ppermute | solution.py:35
  55.2 15.0 %collective-permute-start.7 = (bf16[64,2048]{1,0:T(8,128)(2,1)S(1)}, bf16[64,2048]{1,0:T(8,128)(2,1)S(1)}, u32[]{:S(2)}, u32[]{:S(2)}) collective-permute-start(bf16[64,2048]{1,0:T(8,128)(2,1)S(1)} %add_select_fusion), channel_id=1, source_target_pairs={{0,12},{4,0},{8,4},{12,8},{1,13},{5,1},{9,5},{13,9},{2,14},{6,2},{... | collective-permute-start | bytes 786440 | tf_op jit(solution)/shard_map/ppermute | solution.py:35
  89.9 340.9 %reduce-scatter.2.cloned.1.call-start = ((), (), s32[]{:S(2)}) async-start(), calls=%async_computation.1 | async-start | bytes 17301504 | tf_op jit(solution)/shard_map/reduce_scatter | solution.py:745
  109.4 15.1 %collective-permute-start.14 = (bf16[128,2048]{1,0:T(8,128)(2,1)S(1)}, bf16[128,2048]{1,0:T(8,128)(2,1)S(1)}, u32[]{:S(2)}, u32[]{:S(2)}) collective-permute-start(bf16[128,2048]{1,0:T(8,128)(2,1)S(1)} %get-tuple-element.106), channel_id=1, source_target_pairs={{0,2},{2,64},{64,66},{66,0},{1,3},{3,65},{65,67},{67,1},{4,6},{6,6... | collective-permute-start | bytes 1572872 | tf_op jit(solution)/shard_map/ppermute | solution.py:51
  109.5 25.3 %collective-permute-start.15 = (bf16[128,2048]{1,0:T(8,128)(2,1)S(1)}, bf16[128,2048]{1,0:T(8,128)(2,1)S(1)}, u32[]{:S(2)}, u32[]{:S(2)}) collective-permute-start(bf16[128,2048]{1,0:T(8,128)(2,1)S(1)} %get-tuple-element.107), channel_id=1, source_target_pairs={{0,64},{2,66},{64,0},{66,2},{1,65},{3,67},{65,1},{67,3},{4,68},{6,... | collective-permute-start | bytes 1572872 | tf_op jit(solution)/shard_map/ppermute | solution.py:51
  111.7 23.9 %collective-permute-start.16 = (bf16[128,2048]{1,0:T(8,128)(2,1)S(1)}, bf16[128,2048]{1,0:T(8,128)(2,1)S(1)}, u32[]{:S(2)}, u32[]{:S(2)}) collective-permute-start(bf16[128,2048]{1,0:T(8,128)(2,1)S(1)} %get-tuple-element.108), channel_id=1, source_target_pairs={{0,66},{2,0},{64,2},{66,64},{1,67},{3,1},{65,3},{67,65},{4,70},{6,... | collective-permute-start | bytes 1572872 | tf_op jit(solution)/shard_map/ppermute | solution.py:51
  137.4 14.6 %collective-permute-start.19 = (bf16[128,2048]{1,0:T(8,128)(2,1)S(1)}, bf16[128,2048]{1,0:T(8,128)(2,1)S(1)}, u32[]{:S(2)}, u32[]{:S(2)}) collective-permute-start(bf16[128,2048]{1,0:T(8,128)(2,1)S(1)} %get-tuple-element.110.h0), channel_id=1, source_target_pairs={{0,2},{2,64},{64,66},{66,0},{1,3},{3,65},{65,67},{67,1},{4,6},{6,6... | collective-permute-start | bytes 1572872 | tf_op jit(solution)/shard_map/ppermute | solution.py:35
  139.6 25.1 %collective-permute-start.18 = (bf16[128,2048]{1,0:T(8,128)(2,1)S(1)}, bf16[128,2048]{1,0:T(8,128)(2,1)S(1)}, u32[]{:S(2)}, u32[]{:S(2)}) collective-permute-start(bf16[128,2048]{1,0:T(8,128)(2,1)S(1)} %get-tuple-element.110.h0), channel_id=1, source_target_pairs={{0,64},{2,66},{64,0},{66,2},{1,65},{3,67},{65,1},{67,3},{4,68},{6,... | collective-permute-start | bytes 1572872 | tf_op jit(solution)/shard_map/ppermute | solution.py:35
  141.9 23.7 %collective-permute-start.17 = (bf16[128,2048]{1,0:T(8,128)(2,1)S(1)}, bf16[128,2048]{1,0:T(8,128)(2,1)}, u32[]{:S(2)}, u32[]{:S(2)}) collective-permute-start(bf16[128,2048]{1,0:T(8,128)(2,1)S(1)} %get-tuple-element.110.h0), channel_id=1, source_target_pairs={{0,66},{2,0},{64,2},{66,64},{1,67},{3,1},{65,3},{67,65},{4,70},{6,... | collective-permute-start | bytes 1572872 | tf_op jit(solution)/shard_map/ppermute | solution.py:35
  184.0 13.7 %collective-permute-start.20 = (bf16[128,2048]{1,0:T(8,128)(2,1)}, bf16[128,2048]{1,0:T(8,128)(2,1)S(1)}, u32[]{:S(2)}, u32[]{:S(2)}) collective-permute-start(bf16[128,2048]{1,0:T(8,128)(2,1)} %get-tuple-element.112), channel_id=1, source_target_pairs={{0,2},{2,64},{64,66},{66,0},{1,3},{3,65},{65,67},{67,1},{4,6},{6,6... | collective-permute-start | bytes 1572872 | tf_op jit(solution)/shard_map/ppermute | solution.py:51
  185.0 25.2 %collective-permute-start.21 = (bf16[128,2048]{1,0:T(8,128)(2,1)}, bf16[128,2048]{1,0:T(8,128)(2,1)S(1)}, u32[]{:S(2)}, u32[]{:S(2)}) collective-permute-start(bf16[128,2048]{1,0:T(8,128)(2,1)} %get-tuple-element.113), channel_id=1, source_target_pairs={{0,64},{2,66},{64,0},{66,2},{1,65},{3,67},{65,1},{67,3},{4,68},{6,... | collective-permute-start | bytes 1572872 | tf_op jit(solution)/shard_map/ppermute | solution.py:51
  187.2 23.1 %collective-permute-start.22 = (bf16[128,2048]{1,0:T(8,128)(2,1)}, bf16[128,2048]{1,0:T(8,128)(2,1)S(1)}, u32[]{:S(2)}, u32[]{:S(2)}) collective-permute-start(bf16[128,2048]{1,0:T(8,128)(2,1)} %get-tuple-element.114), channel_id=1, source_target_pairs={{0,66},{2,0},{64,2},{66,64},{1,67},{3,1},{65,3},{67,65},{4,70},{6,... | collective-permute-start | bytes 1572872 | tf_op jit(solution)/shard_map/ppermute | solution.py:51
  215.8 14.5 %collective-permute-start.25 = (bf16[128,2048]{1,0:T(8,128)(2,1)S(1)}, bf16[128,2048]{1,0:T(8,128)(2,1)S(1)}, u32[]{:S(2)}, u32[]{:S(2)}) collective-permute-start(bf16[128,2048]{1,0:T(8,128)(2,1)S(1)} %get-tuple-element.118.g0), channel_id=1, source_target_pairs={{0,2},{2,64},{64,66},{66,0},{1,3},{3,65},{65,67},{67,1},{4,6},{6,6... | collective-permute-start | bytes 1572872 | tf_op jit(solution)/shard_map/ppermute | solution.py:35
  217.8 25.2 %collective-permute-start.24 = (bf16[128,2048]{1,0:T(8,128)(2,1)S(1)}, bf16[128,2048]{1,0:T(8,128)(2,1)S(1)}, u32[]{:S(2)}, u32[]{:S(2)}) collective-permute-start(bf16[128,2048]{1,0:T(8,128)(2,1)S(1)} %get-tuple-element.118.g0), channel_id=1, source_target_pairs={{0,64},{2,66},{64,0},{66,2},{1,65},{3,67},{65,1},{67,3},{4,68},{6,... | collective-permute-start | bytes 1572872 | tf_op jit(solution)/shard_map/ppermute | solution.py:35
  220.3 22.8 %collective-permute-start.23 = (bf16[128,2048]{1,0:T(8,128)(2,1)S(1)}, bf16[128,2048]{1,0:T(8,128)(2,1)S(1)}, u32[]{:S(2)}, u32[]{:S(2)}) collective-permute-start(bf16[128,2048]{1,0:T(8,128)(2,1)S(1)} %get-tuple-element.118.g0), channel_id=1, source_target_pairs={{0,66},{2,0},{64,2},{66,64},{1,67},{3,1},{65,3},{67,65},{4,70},{6,... | collective-permute-start | bytes 1572872 | tf_op jit(solution)/shard_map/ppermute | solution.py:35
  286.2 13.6 %collective-permute-start.26 = (bf16[128,2048]{1,0:T(8,128)(2,1)}, bf16[128,2048]{1,0:T(8,128)(2,1)S(1)}, u32[]{:S(2)}, u32[]{:S(2)}) collective-permute-start(bf16[128,2048]{1,0:T(8,128)(2,1)} %get-tuple-element.121), channel_id=1, source_target_pairs={{0,2},{2,64},{64,66},{66,0},{1,3},{3,65},{65,67},{67,1},{4,6},{6,6... | collective-permute-start | bytes 1572872 | tf_op jit(solution)/shard_map/ppermute | solution.py:51
  286.9 25.4 %collective-permute-start.27 = (bf16[128,2048]{1,0:T(8,128)(2,1)}, bf16[128,2048]{1,0:T(8,128)(2,1)S(1)}, u32[]{:S(2)}, u32[]{:S(2)}) collective-permute-start(bf16[128,2048]{1,0:T(8,128)(2,1)} %get-tuple-element.122), channel_id=1, source_target_pairs={{0,64},{2,66},{64,0},{66,2},{1,65},{3,67},{65,1},{67,3},{4,68},{6,... | collective-permute-start | bytes 1572872 | tf_op jit(solution)/shard_map/ppermute | solution.py:51
  289.4 23.1 %collective-permute-start.28 = (bf16[128,2048]{1,0:T(8,128)(2,1)}, bf16[128,2048]{1,0:T(8,128)(2,1)S(1)}, u32[]{:S(2)}, u32[]{:S(2)}) collective-permute-start(bf16[128,2048]{1,0:T(8,128)(2,1)} %get-tuple-element.123), channel_id=1, source_target_pairs={{0,66},{2,0},{64,2},{66,64},{1,67},{3,1},{65,3},{67,65},{4,70},{6,... | collective-permute-start | bytes 1572872 | tf_op jit(solution)/shard_map/ppermute | solution.py:51
  317.1 14.6 %collective-permute-start.31 = (bf16[128,2048]{1,0:T(8,128)(2,1)S(1)}, bf16[128,2048]{1,0:T(8,128)(2,1)S(1)}, u32[]{:S(2)}, u32[]{:S(2)}) collective-permute-start(bf16[128,2048]{1,0:T(8,128)(2,1)S(1)} %get-tuple-element.126.g0), channel_id=1, source_target_pairs={{0,2},{2,64},{64,66},{66,0},{1,3},{3,65},{65,67},{67,1},{4,6},{6,6... | collective-permute-start | bytes 1572872 | tf_op jit(solution)/shard_map/ppermute | solution.py:35
  318.4 26.2 %collective-permute-start.30 = (bf16[128,2048]{1,0:T(8,128)(2,1)S(1)}, bf16[128,2048]{1,0:T(8,128)(2,1)S(1)}, u32[]{:S(2)}, u32[]{:S(2)}) collective-permute-start(bf16[128,2048]{1,0:T(8,128)(2,1)S(1)} %get-tuple-element.126.g0), channel_id=1, source_target_pairs={{0,64},{2,66},{64,0},{66,2},{1,65},{3,67},{65,1},{67,3},{4,68},{6,... | collective-permute-start | bytes 1572872 | tf_op jit(solution)/shard_map/ppermute | solution.py:35
  321.7 22.9 %collective-permute-start.29 = (bf16[128,2048]{1,0:T(8,128)(2,1)S(1)}, bf16[128,2048]{1,0:T(8,128)(2,1)S(1)}, u32[]{:S(2)}, u32[]{:S(2)}) collective-permute-start(bf16[128,2048]{1,0:T(8,128)(2,1)S(1)} %get-tuple-element.126.g0), channel_id=1, source_target_pairs={{0,66},{2,0},{64,2},{66,64},{1,67},{3,1},{65,3},{67,65},{4,70},{6,... | collective-permute-start | bytes 1572872 | tf_op jit(solution)/shard_map/ppermute | solution.py:35
  354.9 16.5 %collective-permute-start.33 = (bf16[2,512,768]{2,1,0:T(8,128)(2,1)S(1)}, bf16[2,512,768]{2,1,0:T(8,128)(2,1)S(1)}, u32[]{:S(2)}, u32[]{:S(2)}) collective-permute-start(bf16[2,512,768]{2,1,0:T(8,128)(2,1)S(1)} %bitcast.39), channel_id=1, source_target_pairs={{0,1},{1,0},{2,3},{3,2},{4,5},{5,4},{6,7},{7,6},{8,9},{9,8},{10,11... | collective-permute-start | bytes 4718600 | tf_op jit(solution)/shard_map/ppermute | solution.py:39
  364.9 37.6 %collective-permute-start.43 = (bf16[4,64,2048]{2,1,0:T(8,128)(2,1)S(1)}, bf16[4,64,2048]{2,1,0:T(8,128)(2,1)S(1)}, u32[]{:S(2)}, u32[]{:S(2)}) collective-permute-start(bf16[4,64,2048]{2,1,0:T(8,128)(2,1)S(1)} %get-tuple-element.148), channel_id=1, source_target_pairs={{0,1},{1,0},{2,3},{3,2},{4,5},{5,4},{6,7},{7,6},{8,9},{9,8},{10,11... | collective-permute-start | bytes 3145736 | tf_op jit(solution)/shard_map/ppermute | solution.py:39
  365.1 20.4 %collective-permute-start.40 = (bf16[4,128,384]{2,1,0:T(8,128)(2,1)S(1)}, bf16[4,128,384]{2,1,0:T(8,128)(2,1)S(1)}, u32[]{:S(2)}, u32[]{:S(2)}) collective-permute-start(bf16[4,128,384]{2,1,0:T(8,128)(2,1)S(1)} %get-tuple-element.142), channel_id=1, source_target_pairs={{0,4},{4,8},{8,12},{12,0},{1,5},{5,9},{9,13},{13,1},{2,6},{6,10},{... | collective-permute-start | bytes 1179656 | tf_op jit(solution)/shard_map/ppermute | solution.py:51
  365.7 30.0 %collective-permute-start.41 = (bf16[4,128,384]{2,1,0:T(8,128)(2,1)S(1)}, bf16[4,128,384]{2,1,0:T(8,128)(2,1)S(1)}, u32[]{:S(2)}, u32[]{:S(2)}) collective-permute-start(bf16[4,128,384]{2,1,0:T(8,128)(2,1)S(1)} %get-tuple-element.143), channel_id=1, source_target_pairs={{0,8},{4,12},{8,0},{12,4},{1,9},{5,13},{9,1},{13,5},{2,10},{6,14},... | collective-permute-start | bytes 1179656 | tf_op jit(solution)/shard_map/ppermute | solution.py:51
  369.3 30.0 %collective-permute-start.42 = (bf16[4,128,384]{2,1,0:T(8,128)(2,1)S(1)}, bf16[4,128,384]{2,1,0:T(8,128)(2,1)S(1)}, u32[]{:S(2)}, u32[]{:S(2)}) collective-permute-start(bf16[4,128,384]{2,1,0:T(8,128)(2,1)S(1)} %get-tuple-element.144), channel_id=1, source_target_pairs={{0,12},{4,0},{8,4},{12,8},{1,13},{5,1},{9,5},{13,9},{2,14},{6,2},{... | collective-permute-start | bytes 1179656 | tf_op jit(solution)/shard_map/ppermute | solution.py:51
  371.3 30.3 %collective-permute-start.37 = (bf16[4,144,384]{2,1,0:T(8,128)(2,1)S(1)}, bf16[4,144,384]{2,1,0:T(8,128)(2,1)S(1)}, u32[]{:S(2)}, u32[]{:S(2)}) collective-permute-start(bf16[4,144,384]{2,1,0:T(8,128)(2,1)S(1)} %get-tuple-element.138), channel_id=1, source_target_pairs={{0,16},{16,32},{32,48},{48,0},{1,17},{17,33},{33,49},{49,1},{2,18}... | collective-permute-start | bytes 1327112 | tf_op jit(solution)/shard_map/ppermute | solution.py:51
  385.5 31.2 %collective-permute-start.34 = (bf16[128,2048]{1,0:T(8,128)(2,1)S(1)}, bf16[128,2048]{1,0:T(8,128)(2,1)S(1)}, u32[]{:S(2)}, u32[]{:S(2)}) collective-permute-start(bf16[128,2048]{1,0:T(8,128)(2,1)S(1)} %get-tuple-element.134), channel_id=1, source_target_pairs={{0,2},{2,64},{64,66},{66,0},{1,3},{3,65},{65,67},{67,1},{4,6},{6,6... | collective-permute-start | bytes 1572872 | tf_op jit(solution)/shard_map/ppermute | solution.py:51
  396.5 20.2 %collective-permute-start.35 = (bf16[128,2048]{1,0:T(8,128)(2,1)S(1)}, bf16[128,2048]{1,0:T(8,128)(2,1)S(1)}, u32[]{:S(2)}, u32[]{:S(2)}) collective-permute-start(bf16[128,2048]{1,0:T(8,128)(2,1)S(1)} %get-tuple-element.135), channel_id=1, source_target_pairs={{0,64},{2,66},{64,0},{66,2},{1,65},{3,67},{65,1},{67,3},{4,68},{6,... | collective-permute-start | bytes 1572872 | tf_op jit(solution)/shard_map/ppermute | solution.py:51
  399.3 16.6 %collective-permute-start.38 = (bf16[4,144,384]{2,1,0:T(8,128)(2,1)S(1)}, bf16[4,144,384]{2,1,0:T(8,128)(2,1)S(1)}, u32[]{:S(2)}, u32[]{:S(2)}) collective-permute-start(bf16[4,144,384]{2,1,0:T(8,128)(2,1)S(1)} %get-tuple-element.139), channel_id=1, source_target_pairs={{0,32},{16,48},{32,0},{48,16},{1,33},{17,49},{33,1},{49,17},{2,34}... | collective-permute-start | bytes 1327112 | tf_op jit(solution)/shard_map/ppermute | solution.py:51
  401.6 30.8 %collective-permute-start.36 = (bf16[128,2048]{1,0:T(8,128)(2,1)}, bf16[128,2048]{1,0:T(8,128)(2,1)}, u32[]{:S(2)}, u32[]{:S(2)}) collective-permute-start(bf16[128,2048]{1,0:T(8,128)(2,1)} %get-tuple-element.136), channel_id=1, source_target_pairs={{0,66},{2,0},{64,2},{66,64},{1,67},{3,1},{65,3},{67,65},{4,70},{6,... | collective-permute-start | bytes 1572872 | tf_op jit(solution)/shard_map/ppermute | solution.py:51
  402.5 32.9 %collective-permute-start.39 = (bf16[4,144,384]{2,1,0:T(8,128)(2,1)}, bf16[4,144,384]{2,1,0:T(8,128)(2,1)}, u32[]{:S(2)}, u32[]{:S(2)}) collective-permute-start(bf16[4,144,384]{2,1,0:T(8,128)(2,1)} %get-tuple-element.140), channel_id=1, source_target_pairs={{0,48},{16,0},{32,16},{48,32},{1,49},{17,1},{33,17},{49,33},{2,50}... | collective-permute-start | bytes 1327112 | tf_op jit(solution)/shard_map/ppermute | solution.py:51
  416.7 18.7 %collective-permute-start.44 = (bf16[64,2048]{1,0:T(8,128)(2,1)}, bf16[64,2048]{1,0:T(8,128)(2,1)}, u32[]{:S(2)}, u32[]{:S(2)}) collective-permute-start(bf16[64,2048]{1,0:T(8,128)(2,1)} %get-tuple-element.150), channel_id=1, source_target_pairs={{0,4},{4,8},{8,12},{12,0},{1,5},{5,9},{9,13},{13,1},{2,6},{6,10},{... | collective-permute-start | bytes 786440 | tf_op jit(solution)/shard_map/ppermute | solution.py:51
  416.7 18.7 %collective-permute-start.45 = (bf16[64,2048]{1,0:T(8,128)(2,1)}, bf16[64,2048]{1,0:T(8,128)(2,1)}, u32[]{:S(2)}, u32[]{:S(2)}) collective-permute-start(bf16[64,2048]{1,0:T(8,128)(2,1)} %get-tuple-element.151), channel_id=1, source_target_pairs={{0,8},{4,12},{8,0},{12,4},{1,9},{5,13},{9,1},{13,5},{2,10},{6,14},... | collective-permute-start | bytes 786440 | tf_op jit(solution)/shard_map/ppermute | solution.py:51
  416.7 18.7 %collective-permute-start.46 = (bf16[64,2048]{1,0:T(8,128)(2,1)}, bf16[64,2048]{1,0:T(8,128)(2,1)}, u32[]{:S(2)}, u32[]{:S(2)}) collective-permute-start(bf16[64,2048]{1,0:T(8,128)(2,1)} %get-tuple-element.152), channel_id=1, source_target_pairs={{0,12},{4,0},{8,4},{12,8},{1,13},{5,1},{9,5},{13,9},{2,14},{6,2},{... | collective-permute-start | bytes 786440 | tf_op jit(solution)/shard_map/ppermute | solution.py:51
  432.4 29.9 %collective-permute-start.57 = (bf16[96,2048]{1,0:T(8,128)(2,1)S(1)}, bf16[96,2048]{1,0:T(8,128)(2,1)S(1)}, u32[]{:S(2)}, u32[]{:S(2)}) collective-permute-start(bf16[96,2048]{1,0:T(8,128)(2,1)S(1)} %get-tuple-element.167), channel_id=1, source_target_pairs={{0,64},{2,66},{64,0},{66,2},{1,65},{3,67},{65,1},{67,3},{4,68},{6,... | collective-permute-start | bytes 1179656 | tf_op jit(solution)/shard_map/ppermute | solution.py:871
  440.6 12.7 %collective-permute-start.58 = (bf16[32,2048]{1,0:T(8,128)(2,1)S(1)}, bf16[32,2048]{1,0:T(8,128)(2,1)S(1)}, u32[]{:S(2)}, u32[]{:S(2)}) collective-permute-start(bf16[32,2048]{1,0:T(8,128)(2,1)S(1)} %get-tuple-element.166), channel_id=1, source_target_pairs={{0,66},{2,64},{64,2},{66,0},{1,67},{3,65},{65,3},{67,1},{4,70},{6,... | collective-permute-start | bytes 393224 | tf_op jit(solution)/shard_map/ppermute | solution.py:872
  449.4 17.0 %collective-permute-start.55 = (bf16[64,2048]{1,0:T(8,128)(2,1)S(1)}, bf16[64,2048]{1,0:T(8,128)(2,1)S(1)}, u32[]{:S(2)}, u32[]{:S(2)}) collective-permute-start(bf16[64,2048]{1,0:T(8,128)(2,1)S(1)} %get-tuple-element.161.refs_8_), channel_id=1, source_target_pairs={{16,0},{34,18},{112,96},{66,114},{17,1},{35,19},{113,97},{67,115},... | collective-permute-start | bytes 786440 | tf_op jit(solution)/shard_map/ppermute | solution.py:61
  450.7 15.7 %collective-permute-start.54 = (bf16[64,2048]{1,0:T(8,128)(2,1)S(1)}, bf16[64,2048]{1,0:T(8,128)(2,1)S(1)}, u32[]{:S(2)}, u32[]{:S(2)}) collective-permute-start(bf16[64,2048]{1,0:T(8,128)(2,1)S(1)} %get-tuple-element.161.refs_8_), channel_id=1, source_target_pairs={{32,0},{50,18},{64,96},{82,114},{33,1},{51,19},{65,97},{83,115},{3... | collective-permute-start | bytes 786440 | tf_op jit(solution)/shard_map/ppermute | solution.py:61
  452.0 15.0 %collective-permute-start.53 = (bf16[64,2048]{1,0:T(8,128)(2,1)S(1)}, bf16[64,2048]{1,0:T(8,128)(2,1)S(1)}, u32[]{:S(2)}, u32[]{:S(2)}) collective-permute-start(bf16[64,2048]{1,0:T(8,128)(2,1)S(1)} %get-tuple-element.161.refs_8_), channel_id=1, source_target_pairs={{48,0},{2,18},{80,96},{98,114},{49,1},{3,19},{81,97},{99,115},{52,... | collective-permute-start | bytes 786440 | tf_op jit(solution)/shard_map/ppermute | solution.py:61
  474.5 11.1 %collective-permute-start.62 = (bf16[48,768]{1,0:T(8,128)(2,1)S(1)}, bf16[48,768]{1,0:T(8,128)(2,1)S(1)}, u32[]{:S(2)}, u32[]{:S(2)}) collective-permute-start(bf16[48,768]{1,0:T(8,128)(2,1)S(1)} %get-tuple-element.173), channel_id=1, source_target_pairs={{0,64},{1,65},{2,66},{3,67},{64,0},{65,1},{66,2},{67,3},{4,68},{5,... | collective-permute-start | bytes 221192 | tf_op jit(solution)/shard_map/ppermute | solution.py:898
  477.8 14.6 %collective-permute-start.67 = (bf16[32,2048]{1,0:T(8,128)(2,1)S(1)}, bf16[32,2048]{1,0:T(8,128)(2,1)S(1)}, u32[]{:S(2)}, u32[]{:S(2)}) collective-permute-start(bf16[32,2048]{1,0:T(8,128)(2,1)S(1)} %get-tuple-element.177.refs_8_), channel_id=1, source_target_pairs={{0,64},{18,82},{96,32},{114,50},{1,65},{19,83},{97,33},{115,51},{4... | collective-permute-start | bytes 393224 | tf_op jit(solution)/shard_map/ppermute | solution.py:69
  (79 other events, 697.5 us)
Sparse Core Ops, SparseCore 0:
  21.7 62.1 all-gather.4
  90.0 74.4 all-gather.6
  286.4 144.3 reduce-scatter.1
